TPU v7x, 128 devices: a whole 4x4x4 slice. The times are simulated.
128 devices in a mesh: row: 8 (over z_hi, x), col: 16 (over z_lo, y, core).
Axes of the slice: x: 4, y: 4, z: 4 (z_hi: 2, z_lo: 2; z = z_hi * 2 + z_lo), core: 2. Of those that a mesh axis runs over, the one named last changes fastest.
Arguments:
- grad_codes: bfloat16 [16384, 3584], P(('row', 'col')), may hold values from -448 to 448
- grad_scales: bfloat16 [16384, 28], P(('row', 'col')), may hold values from 0.0039978027 to 0.039794922
- expert_ids: int32 [16384, 8], P(('row', 'col')), may hold values from 0 to 63, as said below
- slots: int32 [16384, 8], P(('row', 'col')), may hold values from 0 to 15, as said below
- gate_probs: float32 [16384, 8], P(('row', 'col')), may hold values from 0.05 to 0.5
- gate_act: bfloat16 [128, 2048, 512], P(('row', 'col')), may hold values from -6 to 6
- up_act: bfloat16 [128, 2048, 512], P(('row', 'col')), may hold values from -6 to 6
- gate_weight: bfloat16 [128, 3584, 512], P(('row', 'col')), may hold values from -0.09375 to 0.09375
- up_weight: bfloat16 [128, 3584, 512], P(('row', 'col')), may hold values from -0.09375 to 0.09375
- down_weight: bfloat16 [128, 512, 3584], P(('row', 'col')), may hold values from -0.1875 to 0.1875
Outputs:
- token_grad: bfloat16 [16384, 3584], P(('row', 'col'))
Inputs may be any that keep to these rules, and one draw needn't show every extreme that they name: `expert_ids`: each token names 8 different experts, and the 128 tokens of one device name every expert exactly 16 times. On each device the experts fall into 8 sets of equal size, and column k of a token names an expert of set k. slots[t, k] is the number of earlier copies of the same device, in order of token and then of choice, that name the same expert; the copies of one device to one expert hold the slots 0 to 15, each once.
All inputs are finite; a program needn't handle non-finite values.
Results may differ from a plain program's by a relative error of at most 0.0064.
Values may be sent and summed in bfloat16 or wider, within the bound.
No kernel may reach another device: no remote copies, remote signals or barrier semaphores. Data moves between devices by JAX's collectives and lax.ppermute only.
A program may use at most 192 MiB of HBM per device.

v0:
```python
import jax
import jax.numpy as jnp
from jax import lax
from jax.sharding import PartitionSpec as P

GROUP = 2


def contract(left, right):
    return lax.dot_general(
        left, right, (((1,), (1,)), ((), ())), preferred_element_type=jnp.float32
    )


def shards(
    grad_codes,
    grad_scales,
    expert_ids,
    slots,
    gate_probs,
    gate_act,
    up_act,
    gate_weight,
    up_weight,
    down_weight,
):
    token_count, features = grad_codes.shape
    top_count = expert_ids.shape[1]
    blocks = grad_scales.shape[1]
    row_count = lax.axis_size("row")
    col_count = lax.axis_size("col")
    devices = row_count * col_count
    experts = devices // GROUP
    copies = token_count * top_count
    per_pair = copies // experts
    holder = jnp.arange(copies, dtype=jnp.int32) // top_count
    places = expert_ids.reshape(copies) * per_pair + slots.reshape(copies)
    source = jnp.zeros((copies,), jnp.int32).at[places].set(holder)
    picked_codes = jnp.take(grad_codes, source, axis=0).reshape(experts, 1, per_pair, features)
    picked_scales = jnp.take(grad_scales, source, axis=0).reshape(experts, 1, per_pair, blocks)
    send_codes = jnp.broadcast_to(picked_codes, (experts, GROUP, per_pair, features))
    send_scales = jnp.broadcast_to(picked_scales, (experts, GROUP, per_pair, blocks))
    gate_pre = gate_act[0].astype(jnp.float32)
    up_pre = up_act[0].astype(jnp.float32)
    sigmoid_gate = jax.nn.sigmoid(gate_pre)
    arrived_codes, arrived_scales = (
        lax.all_to_all(
            send_codes.reshape(devices, per_pair, features),
            ("row", "col"),
            split_axis=0,
            concat_axis=0,
            tiled=True,
        ),
        lax.all_to_all(
            send_scales.reshape(devices, per_pair, blocks),
            ("row", "col"),
            split_axis=0,
            concat_axis=0,
            tiled=True,
        ),
    )
    expert_rows = devices * per_pair
    grad_rows = (
        (
            arrived_codes.reshape(expert_rows, blocks, features // blocks).astype(jnp.float32)
            * arrived_scales.reshape(expert_rows, blocks, 1).astype(jnp.float32)
        )
        .reshape(expert_rows, features)
        .astype(jnp.bfloat16)
    )
    hidden_grad = contract(grad_rows, down_weight[0])
    gate_grad = (
        hidden_grad * up_pre * sigmoid_gate * (1.0 + gate_pre * (1.0 - sigmoid_gate))
    ).astype(jnp.bfloat16)
    up_grad = (hidden_grad * gate_pre * sigmoid_gate).astype(jnp.bfloat16)
    part_grad = (contract(gate_grad, gate_weight[0]) + contract(up_grad, up_weight[0])).astype(
        jnp.bfloat16
    )
    returned = lax.all_to_all(
        part_grad.reshape(devices, per_pair, features),
        ("row", "col"),
        split_axis=0,
        concat_axis=0,
        tiled=True,
    )
    members = returned.reshape(experts, GROUP, per_pair, features)
    token_grad = jnp.zeros((token_count, features), jnp.float32)
    for member in range(GROUP):
        flat_part = members[:, member].reshape(copies, features)
        chosen = jnp.take(flat_part, places, axis=0).reshape(token_count, top_count, features)
        token_grad = token_grad + jnp.sum(
            chosen.astype(jnp.float32) * gate_probs[:, :, None], axis=1
        )
    return token_grad.astype(jnp.bfloat16)


def solution(mesh):
    placed = (
        P(("row", "col"), None),
        P(("row", "col"), None),
        P(("row", "col"), None),
        P(("row", "col"), None),
        P(("row", "col"), None),
        P(("row", "col"), None, None),
        P(("row", "col"), None, None),
        P(("row", "col"), None, None),
        P(("row", "col"), None, None),
        P(("row", "col"), None, None),
    )
    return jax.shard_map(
        shards, mesh=mesh, in_specs=placed, out_specs=P(("row", "col"), None), check_vma=False
    )
```

profile of v0, /device:TPU:4, one launch (start us, length us, event | category | flops | bytes accessed | tf_op | source)
XLA Modules:
  0.0 654.0 jit_solution(8929505832051621403)
XLA Ops:
  0.0 0.0 copy-start
  0.0 0.8 multiply_add_fusion
  0.8 0.1 copy.15
  0.9 0.1 add.61
  1.0 4.3 scatter_custom_fusion
  5.4 0.1 broadcast_in_dim.46
  5.4 0.8 copy.17
  6.3 3.2 gather_fusion.1
  9.5 0.2 broadcast_select_fusion.1
  9.7 0.1 broadcast_in_dim.53
  9.8 1.2 reshape.185
  11.0 10.5 %all-to-all-start.1 = ((bf16[128,2,224]{2,1,0:T(2,128)(2,1)}), bf16[128,2,224]{2,1,0:T(2,128)(2,1)S(1)}, u32[]{:S(2)}, u32[]{:S(2)}) async-start(bf16[128,2,224]{2,1,0:T(2,128)(2,1)} %reshape.185), calls=%async_computation.1 | async-start | bytes 262144 | tf_op jit(solution)/shard_map/all_to_all | solution.py:54
  21.5 0.0 copy-done
  21.5 7.3 %gather_fusion = bf16[1024,3584]{1,0:T(8,128)(2,1)} fusion(bf16[128,3584]{1,0:T(8,128)(2,1)S(1)} %copy-done, s32[1024]{0:T(1024)S(1)} %fusion.26), kind=kCustom, calls=%fused_computation.2 | custom fusion | bytes 14684160 | tf_op jit(solution)/shard_map/jit(_take)/gather | solution.py:39
  28.8 6.7 %broadcast_select_fusion = bf16[64,16,3584]{2,1,0:T(8,128)(2,1)} fusion(bf16[64,16,3584]{2,1,0:T(8,128)(2,1)} %bitcast.52, pred[64,16]{1,0:T(8,128)(4,1)S(1)} %broadcast_in_dim.46), kind=kLoop, calls=%fused_computation.11 | loop fusion | flops 3670016 | bytes 14681088 | tf_op jit(solution)/shard_map/jit(_take)/select_n | solution.py:39
  35.5 0.0 all-to-all-done.1
  35.5 9.8 %broadcast_in_dim.50 = bf16[64,2,16,3584]{3,2,1,0:T(8,128)(2,1)} broadcast(bf16[64,16,3584]{2,1,0:T(8,128)(2,1)} %broadcast_select_fusion), dimensions={0,2,3} | broadcast | bytes 22020096 | tf_op jit(solution)/shard_map/broadcast_in_dim | solution.py:41
  45.3 10.2 %all-to-all-start = ((bf16[128,16,3584]{2,1,0:T(8,128)(2,1)}), bf16[128,16,3584]{2,1,0:T(8,128)(2,1)}, u32[]{:S(2)}, u32[]{:S(2)}) async-start(bf16[128,16,3584]{2,1,0:T(8,128)(2,1)} %bitcast.51), calls=%async_computation | async-start | bytes 29360128 | tf_op jit(solution)/shard_map/all_to_all | solution.py:47
  55.5 0.4 reshape.186
  55.9 0.1 bitcast_convert_fusion
  56.0 206.8 %all-to-all-done = bf16[128,16,3584]{2,1,0:T(8,128)(2,1)} async-done(((bf16[128,16,3584]{2,1,0:T(8,128)(2,1)}), bf16[128,16,3584]{2,1,0:T(8,128)(2,1)}, u32[]{:S(2)}, u32[]{:S(2)}) %all-to-all-start) | async-done | bytes 14680096 | tf_op jit(solution)/shard_map/all_to_all | solution.py:47
  262.8 26.1 %reshape.129 = f32[2048,28,128]{2,1,0:T(8,128)} reshape(bf16[128,16,3584]{2,1,0:T(8,128)(2,1)} %all-to-all-done) | data formatting | bytes 44040192 | tf_op jit(solution)/shard_map/convert_element_type | solution.py:65
  288.9 17.8 %multiply_convert_fusion = bf16[2048,28,128]{2,1,0:T(8,128)(2,1)} fusion(f32[2048,28,128]{2,1,0:T(8,128)} %reshape.129, f32[2048,28]{1,0:T(8,128)S(1)} %bitcast_convert_fusion), kind=kLoop, calls=%fused_computation.5 | loop fusion | flops 14680064 | bytes 44269568 | tf_op jit(solution)/shard_map/convert_element_type | solution.py:69
  306.7 23.6 %copy.18 = bf16[2048,28,128]{0,2,1:T(8,128)(2,1)} copy(bf16[2048,28,128]{2,1,0:T(8,128)(2,1)} %multiply_convert_fusion) | data formatting | bytes 29360128 | tf_op jit(solution)/shard_map/convert_element_type | solution.py:69
  330.4 0.0 copy-start.3
  330.4 0.0 copy-start.4
  330.4 13.6 %fusion.14 = f32[2048,512]{1,0:T(8,128)} fusion(bf16[2048,3584]{0,1:T(8,128)(2,1)} %bitcast.54, bf16[1,512,3584]{2,1,0:T(8,128)(2,1)} %param.21), kind=kOutput, calls=%fused_computation.28 | convolution fusion | flops 7516192768 | bytes 22544384 | tf_op jit(solution)/shard_map/dot_general | solution.py:10
  344.0 0.0 copy-done.3
  344.0 0.0 copy-done.4
  344.0 18.9 %fusion.12 = f32[2048,3584]{1,0:T(8,128)} fusion(bf16[1,3584,512]{2,1,0:T(8,128)(2,1)S(1)} %copy-done.3, f32[2048,512]{1,0:T(8,128)} %fusion.14, bf16[1,2048,512]{2,1,0:T(8,128)(2,1)S(1)} %copy-done.4, bf16[1,2048,512]{2,1,0:T(8,128)(2,1)} %param.17), kind=kOutput, calls=%fused_computation.26 | convolution fusion | flops 7528775680 | bytes 41418752 | tf_op jit(solution)/shard_map/dot_general | solution.py:10
  362.9 21.3 %add_convert_fusion = bf16[2048,3584]{1,0:T(8,128)(2,1)} fusion(f32[2048,3584]{1,0:T(8,128)} %fusion.12, bf16[1,3584,512]{2,1,0:T(8,128)(2,1)} %param.20, f32[2048,512]{1,0:T(8,128)} %fusion.14, bf16[1,2048,512]{2,1,0:T(8,128)(2,1)} %param.17), kind=kOutput, calls=%fused_computation.6 | convolution fusion | flops 7538212864 | bytes 54001664 | tf_op jit(solution)/shard_map/dot_general | solution.py:10
  384.2 0.0 copy-start.2
  384.2 5.8 all-to-all-start.2
  390.0 0.1 add.69
  390.1 0.0 copy-done.2
  390.1 0.1 copy.20
  390.2 203.0 %all-to-all-done.2 = bf16[128,16,3584]{2,1,0:T(8,128)(2,1)} async-done(((bf16[128,16,3584]{2,1,0:T(8,128)(2,1)}), bf16[128,16,3584]{2,1,0:T(8,128)(2,1)}, u32[]{:S(2)}, u32[]{:S(2)}) %all-to-all-start.2) | async-done | bytes 14680096 | tf_op jit(solution)/shard_map/all_to_all | solution.py:79
  593.3 10.3 %fusion.32 = (bf16[64,1,16,3584]{3,2,1,0:T(8,128)(2,1)}, bf16[64,1,16,3584]{3,2,1,0:T(8,128)(2,1)}) fusion(bf16[64,2,16,3584]{3,2,1,0:T(8,128)(2,1)} %bitcast.14), kind=kLoop, calls=%fused_computation.57 | loop fusion | bytes 29360128 | tf_op jit(solution)/shard_map/slice | solution.py:89
  603.6 17.8 %gather_fusion.2 = bf16[1024,3584]{1,0:T(8,128)(2,1)} fusion(bf16[1024,3584]{1,0:T(8,128)(2,1)} %bitcast.50, s32[1024]{0:T(1024)S(1)} %fusion.27), kind=kCustom, calls=%fused_computation.clone | custom fusion | bytes 14684160 | tf_op jit(solution)/shard_map/jit(_take)/gather | solution.py:90
  621.4 17.8 %gather_fusion.3 = bf16[1024,3584]{1,0:T(8,128)(2,1)} fusion(bf16[1024,3584]{1,0:T(8,128)(2,1)} %bitcast.49, s32[1024]{0:T(1024)S(1)} %fusion.27), kind=kCustom, calls=%fused_computation.1.clone | custom fusion | bytes 14684160 | tf_op jit(solution)/shard_map/jit(_take)/gather | solution.py:90
  639.2 0.0 copy-start.1
  639.2 13.7 %fusion = (f32[128,3584]{1,0:T(8,128)S(1)}, f32[128,3584]{1,0:T(8,128)S(1)}) fusion(bf16[1024,3584]{1,0:T(8,128)(2,1)} %gather_fusion.3, f32[128,8]{1,0:T(8,128)S(1)} %copy.20, pred[1024]{0:T(1024)(128)(4,1)S(1)} %compare_and_fusion, bf16[1024,3584]{1,0:T(8,128)(2,1)} %gather_fusion.2), kind=kLoop, calls=%fused_computation.8 | loop fusion | flops 28442624 | bytes 18355200 | tf_op jit(solution)/shard_map/reduce_sum | solution.py:91
  652.9 1.1 add_convert_fusion.1
  654.0 0.0 copy-done.1
  (6 shorter events, 0.0 us)
Async XLA Ops:
  0.0 21.5 %copy-start = (bf16[128,3584]{1,0:T(8,128)(2,1)S(1)}, bf16[128,3584]{1,0:T(8,128)(2,1)}, u32[]{:S(2)}) copy-start(bf16[128,3584]{1,0:T(8,128)(2,1)} %param.12) | copy-start | bytes 2752516
  11.0 24.5 %all-to-all-start.1 = ((bf16[128,2,224]{2,1,0:T(2,128)(2,1)}), bf16[128,2,224]{2,1,0:T(2,128)(2,1)S(1)}, u32[]{:S(2)}, u32[]{:S(2)}) async-start(bf16[128,2,224]{2,1,0:T(2,128)(2,1)} %reshape.185), calls=%async_computation.1 | async-start | bytes 262144 | tf_op jit(solution)/shard_map/all_to_all | solution.py:54
  45.3 217.5 %all-to-all-start = ((bf16[128,16,3584]{2,1,0:T(8,128)(2,1)}), bf16[128,16,3584]{2,1,0:T(8,128)(2,1)}, u32[]{:S(2)}, u32[]{:S(2)}) async-start(bf16[128,16,3584]{2,1,0:T(8,128)(2,1)} %bitcast.51), calls=%async_computation | async-start | bytes 29360128 | tf_op jit(solution)/shard_map/all_to_all | solution.py:47
  330.4 13.6 %copy-start.3 = (bf16[1,3584,512]{2,1,0:T(8,128)(2,1)S(1)}, bf16[1,3584,512]{2,1,0:T(8,128)(2,1)}, u32[]{:S(2)}) copy-start(bf16[1,3584,512]{2,1,0:T(8,128)(2,1)} %param.19) | copy-start | bytes 11010052
  330.4 13.6 %copy-start.4 = (bf16[1,2048,512]{2,1,0:T(8,128)(2,1)S(1)}, bf16[1,2048,512]{2,1,0:T(8,128)(2,1)}, u32[]{:S(2)}) copy-start(bf16[1,2048,512]{2,1,0:T(8,128)(2,1)} %param.18) | copy-start | bytes 6291460
  384.2 5.9 copy-start.2
  384.2 209.1 %all-to-all-start.2 = ((bf16[128,16,3584]{2,1,0:T(8,128)(2,1)}), bf16[128,16,3584]{2,1,0:T(8,128)(2,1)}, u32[]{:S(2)}, u32[]{:S(2)}) async-start(bf16[128,16,3584]{2,1,0:T(8,128)(2,1)} %bitcast.53), calls=%async_computation.2 | async-start | bytes 29360128 | tf_op jit(solution)/shard_map/all_to_all | solution.py:79
  639.2 14.8 %copy-start.1 = (bf16[128,3584]{1,0:T(8,128)(2,1)S(1)}, bf16[128,3584]{1,0:T(8,128)(2,1)}, u32[]{:S(2)}) copy-start(bf16[128,3584]{1,0:T(8,128)(2,1)} %param.12) | copy-start | bytes 2752516
where the time goes:
time: 656 us; the launch traced here: 654 us
  waiting for transfers between devices  410 us (62%)
  local copies, waits for them, and re-layouts  123 us (19%)
  matrix products  53.8 us (8%)
  other arithmetic  40.5 us (6%)
  starting transfers between devices  26.5 us (4%)
    all_to_all x1, waiting for transfers between devices, shards(): lax.all_to_all(send_codes.reshape(devices, per_pair, features), ('row', '...  207 us
    all_to_all x1, waiting for transfers between devices, shards(): lax.all_to_all(part_grad.reshape(devices, per_pair, features), ('row', 'c...  203 us
    dot_general x3, matrix products, contract(): lax.dot_general(left, right, (((1,), (1,)), ((), ())), preferred_element_...  53.8 us
    gather x2, local copies, waits for them, and re-layouts, shards(): jnp.take(flat_part, places, axis=0)  35.6 us
    convert_element_type x1, local copies, waits for them, and re-layouts, shards(): arrived_codes.reshape(expert_rows, blocks, features // blocks)  26.1 us
    convert_element_type x1, local copies, waits for them, and re-layouts, shards(): grad_rows = (arrived_codes.reshape(expert_rows, blocks, features // block...  23.6 us
    convert_element_type x1, other arithmetic, shards(): grad_rows = (arrived_codes.reshape(expert_rows, blocks, features // block...  17.8 us
    reduce_sum x1, other arithmetic, shards(): jnp.sum(chosen.astype(jnp.float32) * gate_probs[:, :, None], axis=1)  13.7 us
  transfers between devices with their start and end apart: 3, of which 2 were waited for; matrix products, arithmetic and copies ran while one was open for 2% of the time, Pallas kernels for 0%

commit v1 on v0

v1 whole, which is shorter than its diff:
```python
import functools

import jax
import jax.numpy as jnp
from jax import lax
from jax.experimental import pallas as pl
from jax.experimental.pallas import tpu as pltpu
from jax.sharding import Mesh
from jax.sharding import PartitionSpec as P

GROUP = 2
CHUNKS = 2
ROW_TILE = 256
VMEM = 56 * 1024 * 1024
SWAP = [(0, 1), (1, 0)]


def dot_nt(left, right):
    return lax.dot_general(
        left, right, (((1,), (1,)), ((), ())), preferred_element_type=jnp.float32
    )


def dot_nn(left, right):
    return jnp.dot(left, right, preferred_element_type=jnp.float32)


def dot_tn(left, right):
    return lax.dot_general(
        left, right, (((0,), (0,)), ((), ())), preferred_element_type=jnp.float32
    )


def place_of(ids_ref, slots_ref, per_chunk, rows):
    slot = slots_ref[...]
    chunk = slot // per_chunk
    return chunk * rows + ids_ref[...] * per_chunk + (slot - chunk * per_chunk)


def pick_kernel(per_chunk, rows, codes_ref, scales_ref, ids_ref, slots_ref, out_ref, grad_ref):
    tile = out_ref.shape[0]
    tokens, features = codes_ref.shape
    blocks = scales_ref.shape[1]
    width = features // blocks
    step = pl.program_id(0)

    @pl.when(step == 0)
    def _():
        for block in range(blocks):
            lanes = slice(block * width, (block + 1) * width)
            grad_ref[:, lanes] = (
                codes_ref[:, lanes].astype(jnp.float32)
                * scales_ref[:, block : block + 1].astype(jnp.float32)
            ).astype(jnp.bfloat16)

    places = place_of(ids_ref, slots_ref, per_chunk, rows)
    row = lax.broadcasted_iota(jnp.int32, (tile, tokens), 0) + step * tile
    hit = jnp.zeros((tile, tokens), jnp.float32)
    for k in range(places.shape[0]):
        hit = jnp.where(row == places[k : k + 1, :], 1.0, hit)
    out_ref[...] = dot_nn(hit.astype(jnp.bfloat16), grad_ref[...]).astype(jnp.bfloat16)


def pick(codes, scales, ids, slots, per_chunk, rows):
    tokens, features = codes.shape
    top = ids.shape[0]
    copies = tokens * top
    whole = lambda shape: pl.BlockSpec(shape, lambda i: (0,) * len(shape))
    tile = ROW_TILE
    return pl.pallas_call(
        functools.partial(pick_kernel, per_chunk, rows),
        grid=(copies // tile,),
        in_specs=[
            whole(codes.shape),
            whole(scales.shape),
            whole(ids.shape),
            whole(slots.shape),
        ],
        out_specs=pl.BlockSpec((tile, features), lambda i: (i, 0)),
        out_shape=jax.ShapeDtypeStruct((copies, features), jnp.bfloat16),
        scratch_shapes=[pltpu.VMEM((tokens, features), jnp.bfloat16)],
        compiler_params=pltpu.CompilerParams(vmem_limit_bytes=VMEM),
        cost_estimate=pl.CostEstimate(
            flops=2 * copies * tokens * features,
            bytes_accessed=2 * features * (copies + tokens),
            transcendentals=0,
        ),
    )(codes, scales, ids, slots)


def expert_kernel(
    rows_ref, gate_own, gate_far, up_own, up_far, dw_own, dw_far, gw_own, gw_far, uw_own, uw_far,
    out_ref,
):
    rows = rows_ref[...]
    total = None
    for gate_ref, up_ref, dw, gw, uw in (
        (gate_own, up_own, dw_own, gw_own, uw_own),
        (gate_far, up_far, dw_far, gw_far, uw_far),
    ):
        hidden = dot_nt(rows, dw[...])
        gate = gate_ref[...].astype(jnp.float32)
        up = up_ref[...].astype(jnp.float32)
        sig = 1.0 / (1.0 + jnp.exp(-gate))
        gate_grad = (hidden * up * sig * (1.0 + gate * (1.0 - sig))).astype(jnp.bfloat16)
        up_grad = (hidden * gate * sig).astype(jnp.bfloat16)
        part = dot_nt(gate_grad, gw[...]) + dot_nt(up_grad, uw[...])
        total = part if total is None else total + part
    out_ref[...] = total.astype(jnp.bfloat16)


def expert(rows, acts, weights):
    count, features = rows.shape
    hidden = acts[0].shape[1]
    tile = ROW_TILE
    by_row = lambda width: pl.BlockSpec((tile, width), lambda i: (i, 0))
    whole = lambda a: pl.BlockSpec(a.shape, lambda i: (0, 0), pipeline_mode=pl.Buffered(1))
    return pl.pallas_call(
        expert_kernel,
        grid=(count // tile,),
        in_specs=[by_row(features)] + [by_row(hidden)] * 4 + [whole(w) for w in weights],
        out_specs=by_row(features),
        out_shape=jax.ShapeDtypeStruct(rows.shape, jnp.bfloat16),
        compiler_params=pltpu.CompilerParams(vmem_limit_bytes=VMEM),
        cost_estimate=pl.CostEstimate(
            flops=2 * 6 * count * features * hidden,
            bytes_accessed=2 * (2 * count * features + 4 * count * hidden + 6 * hidden * features),
            transcendentals=2 * count * hidden,
        ),
    )(rows, *acts, *weights)


def combine_kernel(per_chunk, rows, ids_ref, slots_ref, probs_ref, *refs):
    parts, out_ref = refs[:-1], refs[-1]
    places = place_of(ids_ref, slots_ref, per_chunk, rows)
    tokens = out_ref.shape[0]
    total = None
    for chunk, part_ref in enumerate(parts):
        row = lax.broadcasted_iota(jnp.int32, (rows, tokens), 0) + chunk * rows
        weight = jnp.zeros((rows, tokens), jnp.float32)
        for k in range(places.shape[0]):
            weight = jnp.where(row == places[k : k + 1, :], probs_ref[k : k + 1, :], weight)
        high = weight.astype(jnp.bfloat16)
        low = (weight - high.astype(jnp.float32)).astype(jnp.bfloat16)
        part = part_ref[...]
        term = dot_tn(high, part) + dot_tn(low, part)
        total = term if total is None else total + term
    out_ref[...] = total.astype(jnp.bfloat16)


def combine(ids, slots, probs, parts, tokens, per_chunk):
    rows, features = parts[0].shape
    lanes = features // 7
    whole = lambda a: pl.BlockSpec(a.shape, lambda i: (0, 0))
    return pl.pallas_call(
        functools.partial(combine_kernel, per_chunk, rows),
        grid=(features // lanes,),
        in_specs=[whole(ids), whole(slots), whole(probs)]
        + [pl.BlockSpec((rows, lanes), lambda i: (0, i)) for _ in parts],
        out_specs=pl.BlockSpec((tokens, lanes), lambda i: (0, i)),
        out_shape=jax.ShapeDtypeStruct((tokens, features), jnp.bfloat16),
        compiler_params=pltpu.CompilerParams(vmem_limit_bytes=VMEM),
        cost_estimate=pl.CostEstimate(
            flops=4 * rows * len(parts) * tokens * features,
            bytes_accessed=2 * features * (rows * len(parts) + tokens),
            transcendentals=0,
        ),
    )(ids, slots, probs, *parts)


def shards(
    grad_codes, grad_scales, expert_ids, slots, gate_probs,
    gate_act, up_act, gate_weight, up_weight, down_weight,
):
    token_count, features = grad_codes.shape
    chips = lax.axis_size("row") * lax.axis_size("chip")
    copies = token_count * expert_ids.shape[1]
    per_pair = copies // chips
    per_chunk = per_pair // CHUNKS
    rows = copies // CHUNKS
    hidden = gate_act.shape[2]
    core = lax.axis_index("core")

    ids, slot, probs = expert_ids.T, slots.T, gate_probs.T
    picked = pick(grad_codes, grad_scales, ids, slot, per_chunk, rows)

    exchange = lambda a: lax.all_to_all(a, ("row", "chip"), 0, 0, tiled=True)
    other = lambda a: lax.ppermute(a, "core", SWAP)
    arrived = [
        exchange(picked[c * rows : (c + 1) * rows].reshape(chips, per_chunk, features))
        for c in range(CHUNKS)
    ]
    weights = []
    for w in (down_weight, gate_weight, up_weight):
        weights += [w[0], other(w[0])]
    acts = []
    for act in (gate_act, up_act):
        split = act[0].reshape(chips, GROUP, per_pair, hidden)
        mine = lax.dynamic_index_in_dim(split, core, 1, keepdims=False)
        theirs = lax.dynamic_index_in_dim(split, 1 - core, 1, keepdims=False)
        acts += [mine, other(theirs)]

    returned = []
    for c in range(CHUNKS):
        cut = [
            a[:, c * per_chunk : (c + 1) * per_chunk].reshape(rows, hidden) for a in acts
        ]
        part = expert(arrived[c].reshape(rows, features), cut, weights)
        returned.append(
            exchange(part.reshape(chips, per_chunk, features)).reshape(rows, features)
        )
    return combine(ids, slot, probs, returned, token_count, per_chunk)


def solution(mesh):
    rows, cols = mesh.devices.shape
    fine = Mesh(mesh.devices.reshape(rows, cols // GROUP, GROUP), ("row", "chip", "core"))
    every = ("row", "chip", "core")
    two, three = P(every, None), P(every, None, None)
    return jax.shard_map(
        shards,
        mesh=fine,
        in_specs=(two,) * 5 + (three,) * 5,
        out_specs=two,
        check_vma=False,
    )
```

time: 656 us -> 255 us (0.39)
  waiting for transfers between devices: 410 us -> 96.3 us
  local copies, waits for them, and re-layouts: 123 us -> 13.2 us
  Pallas kernels: 0 us -> 59.4 us
  matrix products: 53.8 us -> 0 us
  blocking collectives: 0 us -> 53.6 us
  other arithmetic: 40.5 us -> 0 us
    all_to_all x3, waiting for transfers between devices: 410 us -> 96.1 us  [shards(): exchange = lambda a: lax.all_to_all(a, ('row', 'chip'), 0, 0, tiled=True)]
    pallas_call x0 -> x4, Pallas kernels: none -> 59.4 us  [the longest x2 44.9 us: expert(): pl.pallas_call(expert_kernel, grid=(count // tile,), in_specs=[by_row(fea...]
    dot_general x3 -> x0, matrix products: 53.8 us -> none  [contract(): lax.dot_general(left, right, (((1,), (1,)), ((), ())), preferred_element_...]
    all_to_all x0 -> x1, blocking collectives: none -> 53.6 us  [shards(): exchange = lambda a: lax.all_to_all(a, ('row', 'chip'), 0, 0, tiled=True)]
    convert_element_type x2 -> x0, local copies, waits for them, and re-layouts: 49.7 us -> none  [the longest x1 26.1 us: shards(): arrived_codes.reshape(expert_rows, blocks, features // blocks)]
    gather x4 -> x0, local copies, waits for them, and re-layouts: 46.1 us -> none  [the longest x2 35.6 us: shards(): jnp.take(flat_part, places, axis=0)]
    convert_element_type x3 -> x0, other arithmetic: 19 us -> none  [the longest x1 17.8 us: shards(): grad_rows = (arrived_codes.reshape(expert_rows, blocks, features // block...]
    reduce_sum x1 -> x0, other arithmetic: 13.7 us -> none  [shards(): jnp.sum(chosen.astype(jnp.float32) * gate_probs[:, :, None], axis=1)]
  transfers between devices with their start and end apart: 3 -> 8, of which waited for: 2 -> 4; matrix products, arithmetic and copies ran while one was open for 2% -> 2% of each run, Pallas kernels for 0% -> 18%
where the time goes in v1:
time: 255 us; the launch traced here: 254 us
  waiting for transfers between devices  96.3 us (38%)
  Pallas kernels  59.4 us (23%)
  blocking collectives  53.6 us (21%)
  starting transfers between devices  31.2 us (12%)
  local copies, waits for them, and re-layouts  13.2 us (5%)
    all_to_all x3, waiting for transfers between devices, shards(): exchange = lambda a: lax.all_to_all(a, ('row', 'chip'), 0, 0, tiled=True)  96.1 us
    all_to_all x1, blocking collectives, shards(): exchange = lambda a: lax.all_to_all(a, ('row', 'chip'), 0, 0, tiled=True)  53.6 us
    pallas_call x2, Pallas kernels, expert(): pl.pallas_call(expert_kernel, grid=(count // tile,), in_specs=[by_row(fea...  44.9 us
    all_to_all x3, starting transfers between devices, shards(): exchange = lambda a: lax.all_to_all(a, ('row', 'chip'), 0, 0, tiled=True)  30.3 us
    pallas_call x1, Pallas kernels, combine(): pl.pallas_call(functools.partial(combine_kernel, per_chunk, rows), grid=(...  8.54 us
    reshape x1, local copies, waits for them, and re-layouts, shards(): picked[c * rows:(c + 1) * rows].reshape(chips, per_chunk, features)  6.65 us
    pallas_call x1, Pallas kernels, pick(): pl.pallas_call(functools.partial(pick_kernel, per_chunk, rows), grid=(cop...  6.03 us
  transfers between devices with their start and end apart: 8, of which 4 were waited for; matrix products, arithmetic and copies ran while one was open for 2% of the time, Pallas kernels for 18%

profile of v1, /device:TPU:4, one launch (start us, length us, event | category | flops | bytes accessed | tf_op | source)
XLA Modules:
  0.0 253.8 jit_solution(8260418365016481977)
XLA Ops:
  0.0 1.4 copy.11.scales_ref
  1.4 6.0 %shard_map.100 = bf16[1024,3584]{1,0:T(8,128)(2,1)} custom-call(bf16[128,3584]{1,0:T(8,128)(2,1)} %codes_ref.1, bf16[128,28]{1,0:T(8,128)(2,1)} %copy.11.scales_ref, s32[8,128]{1,0:T(8,128)} %bitcast.47, s32[8,128]{1,0:T(8,128)} %bitcast.49), custom_call_target="tpu_custom_call" | custom-call | flops 939524096 | bytes 8257536 | tf_op jit(solution)/shard_map/pallas_call | solution.py:70
  7.4 6.6 %slice_bitcast_fusion = (bf16[64,8,3584]{2,1,0:T(8,128)(2,1)}, bf16[64,8,3584]{2,1,0:T(8,128)(2,1)}) fusion(bf16[1024,3584]{1,0:T(8,128)(2,1)} %shard_map.100), kind=kLoop, calls=%fused_computation | loop fusion | bytes 14680064 | tf_op jit(solution)/shard_map/reshape | solution.py:190
  14.1 11.6 %all-to-all-start.2 = ((bf16[64,8,3584]{2,1,0:T(8,128)(2,1)}), bf16[64,8,3584]{2,1,0:T(8,128)(2,1)}, u32[]{:S(2)}, u32[]{:S(2)}) async-start(bf16[64,8,3584]{2,1,0:T(8,128)(2,1)} %get-tuple-element.5), calls=%async_computation.2 | async-start | bytes 7340032 | tf_op jit(solution)/shard_map/all_to_all | solution.py:187
  25.7 0.1 collective-permute-start.2
  25.8 0.5 collective-permute-start.3
  26.3 0.1 collective-permute-start.4
  26.4 49.8 %all-to-all-done.2 = bf16[64,8,3584]{2,1,0:T(8,128)(2,1)} async-done(((bf16[64,8,3584]{2,1,0:T(8,128)(2,1)}), bf16[64,8,3584]{2,1,0:T(8,128)(2,1)}, u32[]{:S(2)}, u32[]{:S(2)}) %all-to-all-start.2) | async-done | bytes 3670048 | tf_op jit(solution)/shard_map/all_to_all | solution.py:187
  76.3 0.0 copy-start
  76.3 10.4 %all-to-all-start = ((bf16[64,8,3584]{2,1,0:T(8,128)(2,1)}), bf16[64,8,3584]{2,1,0:T(8,128)(2,1)}, u32[]{:S(2)}, u32[]{:S(2)}) async-start(bf16[64,8,3584]{2,1,0:T(8,128)(2,1)} %get-tuple-element.6), calls=%async_computation | async-start | bytes 7340032 | tf_op jit(solution)/shard_map/all_to_all | solution.py:187
  86.7 0.0 copy-start.1
  86.7 0.0 copy-done
  86.7 0.2 dynamic-slice_bitcast_fusion
  86.9 0.1 collective-permute-start.1
  87.0 1.3 copy-done.1
  88.3 0.2 dynamic-slice_bitcast_fusion.2
  88.5 0.1 collective-permute-start
  88.6 1.4 slice_bitcast_fusion.3
  90.0 0.0 collective-permute-done.1
  90.0 1.1 slice_bitcast_fusion.2
  91.0 0.2 collective-permute-done
  91.3 1.0 slice_bitcast_fusion.4
  92.3 0.0 collective-permute-done.2.dw_far
  92.3 0.0 collective-permute-done.3.gw_far
  92.3 0.0 collective-permute-done.4.uw_far
  92.3 22.4 %shard_map.102 = bf16[512,3584]{1,0:T(8,128)(2,1)} custom-call(bf16[512,3584]{1,0:T(8,128)(2,1)} %bitcast.21.rows_ref, bf16[512,512]{1,0:T(8,128)(2,1)} %get-tuple-element.20.gate_own, bf16[512,512]{1,0:T(8,128)(2,1)} %get-tuple-element.15.gate_far, bf16[512,512]{1,0:T(8,128)(2,1)} %get-tuple-element.13.up_own, bf16[512,512]{1,0:T(8,128)(2,1)} %get-tuple-element.11.up_far, ...), custom_call_target="tpu_custom_call" | custom-call | flops 11274289152 | bytes 31457280 | tf_op jit(solution)/shard_map/pallas_call | solution.py:118
  114.7 20.2 %all-to-all-done = bf16[64,8,3584]{2,1,0:T(8,128)(2,1)} async-done(((bf16[64,8,3584]{2,1,0:T(8,128)(2,1)}), bf16[64,8,3584]{2,1,0:T(8,128)(2,1)}, u32[]{:S(2)}, u32[]{:S(2)}) %all-to-all-start) | async-done | bytes 3670048 | tf_op jit(solution)/shard_map/all_to_all | solution.py:187
  134.9 8.2 %all-to-all-start.3 = ((bf16[64,8,3584]{2,1,0:T(8,128)(2,1)}), bf16[64,8,3584]{2,1,0:T(8,128)(2,1)}, u32[]{:S(2)}, u32[]{:S(2)}) async-start(bf16[64,8,3584]{2,1,0:T(8,128)(2,1)} %bitcast.43), calls=%async_computation.3 | async-start | bytes 7340032 | tf_op jit(solution)/shard_map/all_to_all | solution.py:187
  143.1 22.5 %shard_map.101 = bf16[512,3584]{1,0:T(8,128)(2,1)} custom-call(bf16[512,3584]{1,0:T(8,128)(2,1)} %bitcast.4.rows_ref, bf16[512,512]{1,0:T(8,128)(2,1)} %get-tuple-element.19.gate_own, bf16[512,512]{1,0:T(8,128)(2,1)} %get-tuple-element.16.gate_far, bf16[512,512]{1,0:T(8,128)(2,1)} %get-tuple-element.14.up_own, bf16[512,512]{1,0:T(8,128)(2,1)} %get-tuple-element.12.up_far, ...), custom_call_target="tpu_custom_call" | custom-call | flops 11274289152 | bytes 31457280 | tf_op jit(solution)/shard_map/pallas_call | solution.py:118
  165.6 26.1 %all-to-all-done.3 = bf16[64,8,3584]{2,1,0:T(8,128)(2,1)} async-done(((bf16[64,8,3584]{2,1,0:T(8,128)(2,1)}), bf16[64,8,3584]{2,1,0:T(8,128)(2,1)}, u32[]{:S(2)}, u32[]{:S(2)}) %all-to-all-start.3) | async-done | bytes 3670048 | tf_op jit(solution)/shard_map/all_to_all | solution.py:187
  191.7 53.6 %all_to_all.20 = bf16[64,8,3584]{2,1,0:T(8,128)(2,1)} all-to-all(bf16[64,8,3584]{2,1,0:T(8,128)(2,1)} %bitcast.44), channel_id=1, replica_groups=mesh['row'=8,'chip'=8,'core'=2] {'row','chip'}, dimensions={0} | all-to-all | bytes 7340032 | tf_op jit(solution)/shard_map/all_to_all | solution.py:187
  245.3 8.5 %shard_map.103 = bf16[128,3584]{1,0:T(8,128)(2,1)} custom-call(s32[8,128]{1,0:T(8,128)} %bitcast.48, s32[8,128]{1,0:T(8,128)} %bitcast.50, f32[8,128]{1,0:T(8,128)} %bitcast.51, bf16[512,3584]{1,0:T(8,128)(2,1)} %bitcast.42, bf16[512,3584]{1,0:T(8,128)(2,1)} %bitcast.27.refs_1_), custom_call_target="tpu_custom_call" | custom-call | flops 1879048192 | bytes 8257536 | tf_op jit(solution)/shard_map/pallas_call | solution.py:155
Async XLA Ops:
  14.1 62.2 %all-to-all-start.2 = ((bf16[64,8,3584]{2,1,0:T(8,128)(2,1)}), bf16[64,8,3584]{2,1,0:T(8,128)(2,1)}, u32[]{:S(2)}, u32[]{:S(2)}) async-start(bf16[64,8,3584]{2,1,0:T(8,128)(2,1)} %get-tuple-element.5), calls=%async_computation.2 | async-start | bytes 7340032 | tf_op jit(solution)/shard_map/all_to_all | solution.py:187
  25.7 66.6 %collective-permute-start.2 = (bf16[512,3584]{1,0:T(8,128)(2,1)}, bf16[512,3584]{1,0:T(8,128)(2,1)}, u32[]{:S(2)}, u32[]{:S(2)}) collective-permute-start(bf16[512,3584]{1,0:T(8,128)(2,1)} %bitcast.52), channel_id=1, source_target_pairs={{0,1},{1,0},{2,3},{3,2},{4,5},{5,4},{6,7},{7,6},{8,9},{9,8},{10,11... | collective-permute-start | bytes 11010056 | tf_op jit(solution)/shard_map/ppermute | solution.py:188
  25.8 66.5 %collective-permute-start.3 = (bf16[3584,512]{1,0:T(8,128)(2,1)}, bf16[3584,512]{1,0:T(8,128)(2,1)}, u32[]{:S(2)}, u32[]{:S(2)}) collective-permute-start(bf16[3584,512]{1,0:T(8,128)(2,1)} %bitcast.55), channel_id=1, source_target_pairs={{0,1},{1,0},{2,3},{3,2},{4,5},{5,4},{6,7},{7,6},{8,9},{9,8},{10,11... | collective-permute-start | bytes 11010056 | tf_op jit(solution)/shard_map/ppermute | solution.py:188
  26.3 66.0 %collective-permute-start.4 = (bf16[3584,512]{1,0:T(8,128)(2,1)}, bf16[3584,512]{1,0:T(8,128)(2,1)}, u32[]{:S(2)}, u32[]{:S(2)}) collective-permute-start(bf16[3584,512]{1,0:T(8,128)(2,1)} %bitcast.58), channel_id=1, source_target_pairs={{0,1},{1,0},{2,3},{3,2},{4,5},{5,4},{6,7},{7,6},{8,9},{9,8},{10,11... | collective-permute-start | bytes 11010056 | tf_op jit(solution)/shard_map/ppermute | solution.py:188
  76.3 10.5 %copy-start = (bf16[1,2048,512]{2,1,0:T(8,128)(2,1)S(1)}, bf16[1,2048,512]{2,1,0:T(8,128)(2,1)}, u32[]{:S(2)}) copy-start(bf16[1,2048,512]{2,1,0:T(8,128)(2,1)} %param.16) | copy-start | bytes 6291460
  76.3 58.6 %all-to-all-start = ((bf16[64,8,3584]{2,1,0:T(8,128)(2,1)}), bf16[64,8,3584]{2,1,0:T(8,128)(2,1)}, u32[]{:S(2)}, u32[]{:S(2)}) async-start(bf16[64,8,3584]{2,1,0:T(8,128)(2,1)} %get-tuple-element.6), calls=%async_computation | async-start | bytes 7340032 | tf_op jit(solution)/shard_map/all_to_all | solution.py:187
  86.7 1.6 copy-start.1
  86.9 3.0 %collective-permute-start.1 = (bf16[64,16,512]{2,1,0:T(8,128)(2,1)S(1)}, bf16[64,16,512]{2,1,0:T(8,128)(2,1)S(1)}, u32[]{:S(2)}, u32[]{:S(2)}) collective-permute-start(bf16[64,16,512]{2,1,0:T(8,128)(2,1)S(1)} %get-tuple-element.7), channel_id=1, source_target_pairs={{0,1},{1,0},{2,3},{3,2},{4,5},{5,4},{6,7},{7,6},{8,9},{9,8},{10,11... | collective-permute-start | bytes 3145736 | tf_op jit(solution)/shard_map/ppermute | solution.py:188
  88.5 2.7 %collective-permute-start = (bf16[64,16,512]{2,1,0:T(8,128)(2,1)S(1)}, bf16[64,16,512]{2,1,0:T(8,128)(2,1)S(1)}, u32[]{:S(2)}, u32[]{:S(2)}) collective-permute-start(bf16[64,16,512]{2,1,0:T(8,128)(2,1)S(1)} %get-tuple-element.9), channel_id=1, source_target_pairs={{0,1},{1,0},{2,3},{3,2},{4,5},{5,4},{6,7},{7,6},{8,9},{9,8},{10,11... | collective-permute-start | bytes 3145736 | tf_op jit(solution)/shard_map/ppermute | solution.py:188
  134.9 56.8 %all-to-all-start.3 = ((bf16[64,8,3584]{2,1,0:T(8,128)(2,1)}), bf16[64,8,3584]{2,1,0:T(8,128)(2,1)}, u32[]{:S(2)}, u32[]{:S(2)}) async-start(bf16[64,8,3584]{2,1,0:T(8,128)(2,1)} %bitcast.43), calls=%async_computation.3 | async-start | bytes 7340032 | tf_op jit(solution)/shard_map/all_to_all | solution.py:187

commit v2 on v0

v2 whole, which is shorter than its diff:
```python
import functools

import jax
import jax.numpy as jnp
import numpy as np
from jax import lax
from jax.experimental import pallas as pl
from jax.experimental.pallas import tpu as pltpu
from jax.sharding import Mesh
from jax.sharding import PartitionSpec as P

GROUP = 2
SIDE = 4
MEMBERS = 8
META = 128
LANES = 512
EARLY = (0, 7, 6, 1)
LATE = (3, 4, 5, 2)
VMEM = 56 * 1024 * 1024


def place_of_chip(chip):
    return (chip // 8) % SIDE, chip % SIDE, chip // 32 * 2 + chip // 4 % 2


def chip_at(x, y, z):
    return ((z // 2 * SIDE + x) * 2 + z % 2) * SIDE + y


def member_of(chip, kind, member):
    place = []
    for axis, at in enumerate(place_of_chip(chip)):
        bit = member >> (2 - axis) & 1
        place.append(((at + kind) ^ bit) - kind & SIDE - 1)
    return chip_at(*place)


def pairs(devices, swapped, member):
    found = []
    for device in range(devices):
        chip, core = divmod(device, GROUP)
        found.append((device, member_of(chip, core ^ swapped, member) * GROUP + core))
    return found


def tables(devices):
    experts, mine, theirs = [], [], []
    for device in range(devices):
        chip, core = divmod(device, GROUP)
        experts.append([member_of(chip, 1 - core, m) for m in range(MEMBERS)])
        for other, blocks in ((core, mine), (1 - core, theirs)):
            blocks.append(
                [
                    member_of(member_of(chip, 1 - other, m), other, g) * GROUP + other
                    for m in EARLY + LATE
                    for g in range(MEMBERS)
                ]
            )
    return [np.array(t, np.int32) for t in (experts, mine, theirs)]


def dot_nt(left, right):
    return lax.dot_general(
        left, right, (((1,), (1,)), ((), ())), preferred_element_type=jnp.float32
    )


def dot_tn(left, right):
    return lax.dot_general(
        left, right, (((0,), (0,)), ((), ())), preferred_element_type=jnp.float32
    )


def dot_nn(left, right):
    return jnp.dot(left, right, preferred_element_type=jnp.float32)


def cost(flops, moved):
    return pl.CostEstimate(flops=flops, bytes_accessed=moved, transcendentals=0)


def split(value):
    high = value.astype(jnp.bfloat16)
    return high, (value - high.astype(jnp.float32)).astype(jnp.bfloat16)


def pack_kernel(codes_ref, scales_ref, ids_ref, slots_ref, probs_ref, out_ref):
    features = codes_ref.shape[1]
    blocks = scales_ref.shape[0]
    width = features // blocks
    scales = scales_ref[...]
    for start in range(0, features, LANES):
        lane = lax.broadcasted_iota(jnp.int32, (blocks, LANES), 1) + start
        block = lax.broadcasted_iota(jnp.int32, (blocks, LANES), 0)
        spread = jnp.where(lane // width == block, 1.0, 0.0).astype(jnp.bfloat16)
        lanes = slice(start, start + LANES)
        out_ref[:, lanes] = (
            codes_ref[:, lanes].astype(jnp.float32) * dot_tn(scales, spread)
        ).astype(jnp.bfloat16)
    high, low = split(probs_ref[...])
    facts = jnp.concatenate(
        [ids_ref[...].astype(jnp.float32), slots_ref[...].astype(jnp.float32),
         high.astype(jnp.float32), low.astype(jnp.float32)], axis=0,
    ).astype(jnp.bfloat16)
    count = facts.shape[0]
    spread = jnp.where(
        lax.broadcasted_iota(jnp.int32, (count, META), 0)
        == lax.broadcasted_iota(jnp.int32, (count, META), 1), 1.0, 0.0,
    ).astype(jnp.bfloat16)
    out_ref[:, features:] = dot_tn(facts, spread).astype(jnp.bfloat16)


def pack(codes, scales, ids, slots, probs):
    tokens, features = codes.shape
    return pl.pallas_call(
        pack_kernel,
        out_shape=jax.ShapeDtypeStruct((tokens, features + META), jnp.bfloat16),
        compiler_params=pltpu.CompilerParams(vmem_limit_bytes=VMEM),
        cost_estimate=cost(2 * tokens * features * scales.shape[0], 4 * tokens * features),
    )(codes, scales, ids, slots, probs)


def wanted(experts_ref, per_pair, rows):
    lane = lax.broadcasted_iota(jnp.int32, (1, rows), 1)
    message = lane // per_pair
    want = jnp.zeros((1, rows), jnp.int32)
    for m in range(MEMBERS):
        want = jnp.where(message == m, experts_ref[m], want)
    return (want * per_pair + (lane - message * per_pair)).astype(jnp.float32)


def places_in(meta, top, per_pair):
    meta = meta.astype(jnp.float32)
    return meta[:, :top] * float(per_pair) + meta[:, top : 2 * top], meta


def pick_kernel(top, per_pair, experts_ref, *refs):
    metas, grads = refs[:MEMBERS], refs[MEMBERS : 2 * MEMBERS]
    outs, hit_ref = refs[2 * MEMBERS : 3 * MEMBERS], refs[-1]
    rows = MEMBERS * per_pair
    tokens = metas[0].shape[0]

    @pl.when(pl.program_id(0) == 0)
    def _():
        want = wanted(experts_ref, per_pair, rows)
        for g in range(MEMBERS):
            place, _ = places_in(metas[g][...], top, per_pair)
            hit = jnp.zeros((tokens, rows), jnp.float32)
            for k in range(top):
                hit = jnp.where(place[:, k : k + 1] == want, 1.0, hit)
            hit_ref[g] = hit.astype(jnp.bfloat16)

    for g in range(MEMBERS):
        picked = dot_tn(hit_ref[g], grads[g][...]).astype(jnp.bfloat16)
        for m in range(MEMBERS):
            outs[m][g * per_pair : (g + 1) * per_pair, :] = picked[m * per_pair : (m + 1) * per_pair, :]


def pick(experts, gathered, features, top, per_pair):
    tokens = gathered[0].shape[0]
    rows = MEMBERS * per_pair
    meta = pl.BlockSpec((tokens, META), lambda i, *_: (0, features // META))
    tile = pl.BlockSpec((tokens, LANES), lambda i, *_: (0, i))
    out = pl.BlockSpec((rows, LANES), lambda i, *_: (0, i))
    return pl.pallas_call(
        functools.partial(pick_kernel, top, per_pair),
        grid_spec=pltpu.PrefetchScalarGridSpec(
            num_scalar_prefetch=1,
            grid=(features // LANES,),
            in_specs=[meta] * MEMBERS + [tile] * MEMBERS,
            out_specs=[out] * MEMBERS,
            scratch_shapes=[pltpu.VMEM((MEMBERS, tokens, rows), jnp.bfloat16)],
        ),
        out_shape=[jax.ShapeDtypeStruct((rows, features), jnp.bfloat16)] * MEMBERS,
        compiler_params=pltpu.CompilerParams(vmem_limit_bytes=VMEM),
        cost_estimate=cost(
            2 * MEMBERS * rows * tokens * features, 2 * MEMBERS * features * (rows + tokens)
        ),
    )(experts, *gathered, *gathered)


def weigh_kernel(top, per_pair, experts_ref, *refs):
    metas, high_ref, low_ref = refs[:MEMBERS], refs[-2], refs[-1]
    rows = MEMBERS * per_pair
    tokens = metas[0].shape[0]
    want = wanted(experts_ref, per_pair, rows)
    for g in range(MEMBERS):
        place, meta = places_in(metas[g][...], top, per_pair)
        high = jnp.zeros((tokens, rows), jnp.float32)
        low = jnp.zeros((tokens, rows), jnp.float32)
        for k in range(top):
            hit = place[:, k : k + 1] == want
            high = jnp.where(hit, meta[:, 2 * top + k : 2 * top + k + 1], high)
            low = jnp.where(hit, meta[:, 3 * top + k : 3 * top + k + 1], low)
        high_ref[g] = high.astype(jnp.bfloat16)
        low_ref[g] = low.astype(jnp.bfloat16)


def weigh(experts, gathered, features, top, per_pair):
    tokens = gathered[0].shape[0]
    rows = MEMBERS * per_pair
    shape = (MEMBERS, tokens, rows)
    meta = pl.BlockSpec((tokens, META), lambda i, *_: (0, features // META))
    out = pl.BlockSpec(shape, lambda i, *_: (0, 0, 0))
    return pl.pallas_call(
        functools.partial(weigh_kernel, top, per_pair),
        grid_spec=pltpu.PrefetchScalarGridSpec(
            num_scalar_prefetch=1, grid=(1,), in_specs=[meta] * MEMBERS, out_specs=[out, out]
        ),
        out_shape=[jax.ShapeDtypeStruct(shape, jnp.bfloat16)] * 2,
        compiler_params=pltpu.CompilerParams(vmem_limit_bytes=VMEM),
        cost_estimate=cost(0, 1 << 22),
    )(experts, *gathered)


def expert_kernel(first, count, *refs):
    messages, refs = refs[:count], refs[count:]
    acts, weights, outs = refs[:4], refs[4:10], refs[10 : 10 + count]
    rows_ref, act_ref, out_ref, in_sem, act_sem, weight_sem, out_sem = refs[10 + count : 17 + count]
    held = refs[17 + count :]
    size = messages[0].shape[0]
    total, features = rows_ref.shape

    rows_in = [
        pltpu.make_async_copy(ref, rows_ref.at[pl.ds(m * size, size)], in_sem.at[m])
        for m, ref in enumerate(messages)
    ]
    acts_in = [
        pltpu.make_async_copy(ref.at[pl.ds(first, total)], act_ref.at[n], act_sem.at[n])
        for n, ref in enumerate(acts)
    ]
    weights_in = [
        pltpu.make_async_copy(ref, held[n], weight_sem.at[n]) for n, ref in enumerate(weights)
    ]
    for copy in rows_in + weights_in[:1] + acts_in[:2] + weights_in[1:2] + acts_in[2:] + weights_in[2:]:
        copy.start()

    for copy in rows_in:
        copy.wait()
    grads = []
    for half in range(GROUP):
        weights_in[half].wait()
        hidden = dot_nt(rows_ref[...], held[half][...])
        acts_in[2 * half].wait()
        acts_in[2 * half + 1].wait()
        gate = act_ref[2 * half].astype(jnp.float32)
        up = act_ref[2 * half + 1].astype(jnp.float32)
        sig = 1.0 / (1.0 + jnp.exp(-gate))
        grads.append((hidden * up * sig * (1.0 + gate * (1.0 - sig))).astype(jnp.bfloat16))
        grads.append((hidden * gate * sig).astype(jnp.bfloat16))
    for copy in weights_in[2:]:
        copy.wait()

    lanes = features // 2
    copies = []
    for part in range(2):
        here = slice(part * lanes, (part + 1) * lanes)
        for start in range(part * lanes, (part + 1) * lanes, lanes // 7):
            cut = slice(start, start + lanes // 7)
            result = dot_nt(grads[0], held[2][cut, :])
            for n in range(1, 4):
                result = result + dot_nt(grads[n], held[2 + n][cut, :])
            out_ref[:, cut] = result.astype(jnp.bfloat16)
        for m, ref in enumerate(outs):
            copy = pltpu.make_async_copy(
                out_ref.at[pl.ds(m * size, size), here], ref.at[:, here], out_sem.at[part, m]
            )
            copy.start()
            copies.append(copy)
    for copy in copies:
        copy.wait()


def expert(first, messages, acts, weights):
    count = len(messages)
    size, features = messages[0].shape
    rows, hidden = count * size, acts[0].shape[1]
    anywhere = pl.BlockSpec(memory_space=pl.ANY)
    return pl.pallas_call(
        functools.partial(expert_kernel, first, count),
        in_specs=[anywhere] * (count + len(acts) + len(weights)),
        out_specs=[anywhere] * count,
        out_shape=[jax.ShapeDtypeStruct((size, features), jnp.bfloat16)] * count,
        scratch_shapes=[
            pltpu.VMEM((rows, features), jnp.bfloat16),
            pltpu.VMEM((len(acts), rows, hidden), jnp.bfloat16),
            pltpu.VMEM((rows, features), jnp.bfloat16),
            pltpu.SemaphoreType.DMA((count,)),
            pltpu.SemaphoreType.DMA((len(acts),)),
            pltpu.SemaphoreType.DMA((len(weights),)),
            pltpu.SemaphoreType.DMA((2, count)),
        ]
        + [pltpu.VMEM(w.shape, jnp.bfloat16) for w in weights],
        compiler_params=pltpu.CompilerParams(vmem_limit_bytes=VMEM),
        cost_estimate=cost(
            12 * rows * features * hidden,
            4 * rows * features + 8 * rows * hidden + 12 * hidden * features,
        ),
    )(*messages, *acts, *weights)


def combine_kernel(per_pair, high_ref, low_ref, *refs):
    messages, outs = refs[:MEMBERS], refs[MEMBERS:]
    for g in range(MEMBERS):
        rows = jnp.concatenate(
            [message[g * per_pair : (g + 1) * per_pair, :] for message in messages], axis=0
        )
        total = dot_nn(high_ref[g], rows) + dot_nn(low_ref[g], rows)
        outs[g][...] = total.astype(outs[g].dtype)


def combine(high, low, messages, per_pair):
    rows, features = messages[0].shape
    tokens = high.shape[1]
    whole = pl.BlockSpec(high.shape, lambda i: (0, 0, 0))
    tile = pl.BlockSpec((rows, LANES), lambda i: (0, i))
    out = pl.BlockSpec((tokens, LANES), lambda i: (0, i))
    return pl.pallas_call(
        functools.partial(combine_kernel, per_pair),
        grid=(features // LANES,),
        in_specs=[whole, whole] + [tile] * MEMBERS,
        out_specs=[out] * MEMBERS,
        out_shape=[
            jax.ShapeDtypeStruct((tokens, features), jnp.float32 if g == 0 else jnp.bfloat16)
            for g in range(MEMBERS)
        ],
        compiler_params=pltpu.CompilerParams(vmem_limit_bytes=VMEM),
        cost_estimate=cost(
            4 * MEMBERS * rows * tokens * features, 2 * MEMBERS * features * (rows + tokens)
        ),
    )(high, low, *messages)


def shards(
    grad_codes, grad_scales, expert_ids, slots, gate_probs,
    gate_act, up_act, gate_weight, up_weight, down_weight,
):
    token_count, features = grad_codes.shape
    top = expert_ids.shape[1]
    devices = lax.axis_size("i")
    per_pair = token_count * top // (devices // GROUP)
    hidden = gate_act.shape[2]
    device = lax.axis_index("i")
    experts, mine, theirs = (
        lax.dynamic_index_in_dim(jnp.asarray(t), device, 0, keepdims=False)
        for t in tables(devices)
    )

    def within(swapped, member, value):
        return lax.ppermute(value, "i", pairs(devices, swapped, member))

    gather = functools.partial(within, 0)
    exchange = functools.partial(within, 1)

    def other(value):
        return lax.ppermute(value, "i", [(d, d ^ 1) for d in range(devices)])

    packed = pack(grad_codes, grad_scales.T, expert_ids.T, slots.T, gate_probs.T)
    got = {0: packed}
    for member in (7, 4, 2, 1):
        got[member] = gather(member, packed)
    for member, axis, first in ((6, 2, 4), (3, 1, 2), (5, 4, 1)):
        got[member] = gather(axis, got[first])
    gathered = [got[m] for m in range(MEMBERS)]

    acts = [[], []]
    for act in (gate_act, up_act):
        blocks = act[0].reshape(devices, per_pair, hidden)
        own, far = (
            blocks.at[at].get(mode="promise_in_bounds").reshape(-1, hidden) for at in (mine, theirs)
        )
        acts[0].append(own)
        acts[1].append(other(far))
    acts = acts[0] + acts[1]
    down, gate, up = down_weight[0], gate_weight[0], up_weight[0]
    weights = [down, other(down), gate, up, other(gate), other(up)]

    messages = pick(experts, gathered, features, top, per_pair)
    high, low = weigh(experts, gathered, features, top, per_pair)
    arrived = {m: exchange(m, messages[m]) if m else messages[m] for m in EARLY + LATE}
    results = {}
    for first, members in ((0, EARLY), (len(EARLY), LATE)):
        parts = expert(
            first * MEMBERS * per_pair, [arrived[m] for m in members], acts, weights
        )
        for m, part in zip(members, parts):
            results[m] = exchange(m, part) if m else part
    sums = combine(high, low, [results[m] for m in range(MEMBERS)], per_pair)
    total = sums[0]
    for m in range(1, MEMBERS):
        total = total + gather(m, sums[m]).astype(jnp.float32)
    return total.astype(jnp.bfloat16)


def solution(mesh):
    flat = Mesh(mesh.devices.reshape(-1), ("i",))
    two, three = P("i", None), P("i", None, None)
    return jax.shard_map(
        shards, mesh=flat, in_specs=(two,) * 5 + (three,) * 5, out_specs=two, check_vma=False
    )
```

time: 656 us -> 261 us (0.40)
  waiting for transfers between devices: 410 us -> 94.9 us
  local copies, waits for them, and re-layouts: 123 us -> 13.9 us
  Pallas kernels: 0 us -> 80.1 us
  matrix products: 53.8 us -> 0 us
  starting transfers between devices: 26.5 us -> 63.2 us
  other arithmetic: 40.5 us -> 4.29 us
    all_to_all x3 -> x0, waiting for transfers between devices: 410 us -> none  [the longest x1 207 us: shards(): lax.all_to_all(send_codes.reshape(devices, per_pair, features), ('row', '...]
    ppermute x0 -> x33, waiting for transfers between devices: none -> 94.9 us  [the longest x28 94.9 us: within(): return lax.ppermute(value, 'i', pairs(devices, swapped, member))]
    pallas_call x0 -> x6, Pallas kernels: none -> 80.1 us  [the longest x2 46.4 us: expert(): pl.pallas_call(functools.partial(expert_kernel, first, count), in_specs=[...]
    ppermute x0 -> x33, starting transfers between devices: none -> 63.2 us  [the longest x28 60.5 us: within(): return lax.ppermute(value, 'i', pairs(devices, swapped, member))]
    dot_general x3 -> x0, matrix products: 53.8 us -> none  [contract(): lax.dot_general(left, right, (((1,), (1,)), ((), ())), preferred_element_...]
    convert_element_type x2 -> x0, local copies, waits for them, and re-layouts: 49.7 us -> none  [the longest x1 26.1 us: shards(): arrived_codes.reshape(expert_rows, blocks, features // blocks)]
    gather x4, local copies, waits for them, and re-layouts: 46.1 us -> 9.65 us  [shards(): blocks.at[at].get(mode='promise_in_bounds').reshape(-1, hidden)]
    all_to_all x3 -> x0, starting transfers between devices: 26.5 us -> none  [the longest x1 10.5 us: shards(): lax.all_to_all(send_scales.reshape(devices, per_pair, blocks), ('row', 'c...]
  transfers between devices with their start and end apart: 3 -> 33, of which waited for: 2 -> 13; matrix products, arithmetic and copies ran while one was open for 2% -> 5% of each run, Pallas kernels for 0% -> 26%
where the time goes in v2:
time: 261 us; the launch traced here: 257 us
  waiting for transfers between devices  94.9 us (36%)
  Pallas kernels  80.1 us (31%)
  starting transfers between devices  63.2 us (24%)
  local copies, waits for them, and re-layouts  13.9 us (5%)
  other arithmetic  4.29 us (2%)
    ppermute x28, waiting for transfers between devices, within(): return lax.ppermute(value, 'i', pairs(devices, swapped, member))  94.9 us
    ppermute x28, starting transfers between devices, within(): return lax.ppermute(value, 'i', pairs(devices, swapped, member))  60.5 us
    pallas_call x2, Pallas kernels, expert(): pl.pallas_call(functools.partial(expert_kernel, first, count), in_specs=[...  46.4 us
    pallas_call x1, Pallas kernels, pick(): pl.pallas_call(functools.partial(pick_kernel, top, per_pair), grid_spec=p...  13.4 us
    pallas_call x1, Pallas kernels, combine(): pl.pallas_call(functools.partial(combine_kernel, per_pair), grid=(feature...  10.3 us
    gather x4, local copies, waits for them, and re-layouts, shards(): blocks.at[at].get(mode='promise_in_bounds').reshape(-1, hidden)  9.65 us
    pallas_call x1, Pallas kernels, weigh(): pl.pallas_call(functools.partial(weigh_kernel, top, per_pair), grid_spec=...  7.2 us
  transfers between devices with their start and end apart: 33, of which 13 were waited for; matrix products, arithmetic and copies ran while one was open for 5% of the time, Pallas kernels for 26%

profile of v2, /device:TPU:4, one launch (start us, length us, event | category | flops | bytes accessed | tf_op | source)
XLA Modules:
  0.0 256.5 jit_solution(3797469388566887863)
XLA Ops:
  0.0 2.8 %shard_map.127.refs_0_.refs_8_ = bf16[128,3712]{1,0:T(8,128)(2,1)} custom-call(bf16[128,3584]{1,0:T(8,128)(2,1)} %codes_ref.1, bf16[28,128]{1,0:T(8,128)(2,1)} %bitcast.41, s32[8,128]{1,0:T(8,128)} %bitcast.42, s32[8,128]{1,0:T(8,128)} %bitcast.43, f32[8,128]{1,0:T(8,128)} %bitcast.44), custom_call_target="tpu_custom_call" | custom-call | flops 25690112 | bytes 1835008 | tf_op jit(solution)/shard_map/pallas_call | solution.py:115
  2.8 1.2 collective-permute-start.3
  4.0 1.6 collective-permute-start.1
  5.5 1.9 collective-permute-start
  7.4 0.3 collective-permute-start.6
  7.7 9.0 %collective-permute-done.3.refs_4_.refs_12_ = bf16[128,3712]{1,0:T(8,128)(2,1)S(1)} collective-permute-done((bf16[128,3712]{1,0:T(8,128)(2,1)}, bf16[128,3712]{1,0:T(8,128)(2,1)S(1)}, u32[]{:S(2)}, u32[]{:S(2)}) %collective-permute-start.3) | collective-permute-done | bytes 950304 | tf_op jit(solution)/shard_map/ppermute | solution.py:350
  16.7 1.6 collective-permute-start.5
  18.3 9.9 %collective-permute-done.1.refs_2_.refs_10_ = bf16[128,3712]{1,0:T(8,128)(2,1)} collective-permute-done((bf16[128,3712]{1,0:T(8,128)(2,1)}, bf16[128,3712]{1,0:T(8,128)(2,1)}, u32[]{:S(2)}, u32[]{:S(2)}) %collective-permute-start.1) | collective-permute-done | bytes 950304 | tf_op jit(solution)/shard_map/ppermute | solution.py:350
  28.2 1.9 collective-permute-start.2
  30.1 0.0 collective-permute-done.refs_1_.refs_9_
  30.1 0.0 collective-permute-start.4
  30.1 2.1 collective-permute-start.13
  32.2 0.1 collective-permute-start.14
  32.3 6.0 %collective-permute-done.5.refs_6_.refs_14_ = bf16[128,3712]{1,0:T(8,128)(2,1)S(1)} collective-permute-done((bf16[128,3712]{1,0:T(8,128)(2,1)S(1)}, bf16[128,3712]{1,0:T(8,128)(2,1)S(1)}, u32[]{:S(2)}, u32[]{:S(2)}) %collective-permute-start.5) | collective-permute-done | bytes 950304 | tf_op jit(solution)/shard_map/ppermute | solution.py:350
  38.3 1.0 copy-done.4
  39.2 0.0 collective-permute-start.12
  39.2 0.7 fusion.3
  40.0 1.6 gather_fusion.3
  41.6 3.2 %gather_fusion.2 = bf16[64,16,512]{2,1,0:T(8,128)(2,1)} fusion(bf16[128,16,512]{2,1,0:T(8,128)(2,1)} %bitcast.33, s32[1024]{0:T(1024)S(1)} %pad_clamp_fusion), kind=kCustom, calls=%fused_computation.2 | custom fusion | bytes 2097408 | tf_op jit(solution)/shard_map/gather | solution.py:370
  44.8 0.0 collective-permute-done.2.refs_3_.refs_11_
  44.8 0.5 collective-permute-start.10
  45.3 0.0 collective-permute-done.4.refs_5_.refs_13_
  45.3 0.1 collective-permute-start.11
  45.4 1.3 fusion.experts_ref
  46.7 13.4 %shard_map.129 = (bf16[128,3584]{1,0:T(8,128)(2,1)}, bf16[128,3584]{1,0:T(8,128)(2,1)}, bf16[128,3584]{1,0:T(8,128)(2,1)}, bf16[128,3584]{1,0:T(8,128)(2,1)}, bf...) custom-call(s32[8]{0:T(128)} %fusion.experts_ref, ...), custom_call_target="tpu_custom_call" | custom-call | flops 939524096 | bytes 14680064 | tf_op jit(solution)/shard_map/pallas_call | solution.py:165
  60.2 6.6 %collective-permute-start.16 = (bf16[128,3584]{1,0:T(8,128)(2,1)}, bf16[128,3584]{1,0:T(8,128)(2,1)S(1)}, u32[]{:S(2)}, u32[]{:S(2)}) collective-permute-start(bf16[128,3584]{1,0:T(8,128)(2,1)} %get-tuple-element.39), channel_id=1, source_target_pairs={{0,78},{1,11},{2,76},{3,9},{4,74},{5,15},{6,72},{7,13},{8,70},{9,3... | collective-permute-start | bytes 2752520 | tf_op jit(solution)/shard_map/ppermute | solution.py:350
  66.7 0.4 collective-permute-start.17
  67.1 11.2 %collective-permute-done.16.refs_0_ = bf16[128,3584]{1,0:T(8,128)(2,1)S(1)} collective-permute-done((bf16[128,3584]{1,0:T(8,128)(2,1)}, bf16[128,3584]{1,0:T(8,128)(2,1)S(1)}, u32[]{:S(2)}, u32[]{:S(2)}) %collective-permute-start.16) | collective-permute-done | bytes 917536 | tf_op jit(solution)/shard_map/ppermute | solution.py:350
  78.3 2.8 %collective-permute-start.18 = (bf16[128,3584]{1,0:T(8,128)(2,1)}, bf16[128,3584]{1,0:T(8,128)(2,1)}, u32[]{:S(2)}, u32[]{:S(2)}) collective-permute-start(bf16[128,3584]{1,0:T(8,128)(2,1)} %get-tuple-element.41), channel_id=1, source_target_pairs={{0,120},{1,25},{2,122},{3,27},{4,124},{5,29},{6,126},{7,31},{8,112... | collective-permute-start | bytes 2752520 | tf_op jit(solution)/shard_map/ppermute | solution.py:350
  81.1 2.9 %collective-permute-start.19 = (bf16[128,3584]{1,0:T(8,128)(2,1)}, bf16[128,3584]{1,0:T(8,128)(2,1)}, u32[]{:S(2)}, u32[]{:S(2)}) collective-permute-start(bf16[128,3584]{1,0:T(8,128)(2,1)} %get-tuple-element.42), channel_id=1, source_target_pairs={{0,6},{1,3},{2,4},{3,1},{4,2},{5,7},{6,0},{7,5},{8,14},{9,11},{10,... | collective-permute-start | bytes 2752520 | tf_op jit(solution)/shard_map/ppermute | solution.py:350
  84.1 1.6 gather_fusion.1
  85.7 3.2 %gather_fusion = bf16[64,16,512]{2,1,0:T(8,128)(2,1)} fusion(bf16[128,16,512]{2,1,0:T(8,128)(2,1)} %bitcast.34, s32[1024]{0:T(1024)S(1)} %pad_clamp_fusion.1), kind=kCustom, calls=%fused_computation | custom fusion | bytes 2097408 | tf_op jit(solution)/shard_map/gather | solution.py:370
  88.9 5.3 %collective-permute-done.18.refs_2_ = bf16[128,3584]{1,0:T(8,128)(2,1)} collective-permute-done((bf16[128,3584]{1,0:T(8,128)(2,1)}, bf16[128,3584]{1,0:T(8,128)(2,1)}, u32[]{:S(2)}, u32[]{:S(2)}) %collective-permute-start.18) | collective-permute-done | bytes 917536 | tf_op jit(solution)/shard_map/ppermute | solution.py:350
  94.1 5.1 %collective-permute-start.7 = (bf16[128,3584]{1,0:T(8,128)(2,1)}, bf16[128,3584]{1,0:T(8,128)(2,1)S(1)}, u32[]{:S(2)}, u32[]{:S(2)}) collective-permute-start(bf16[128,3584]{1,0:T(8,128)(2,1)} %get-tuple-element.34), channel_id=1, source_target_pairs={{0,126},{1,27},{2,124},{3,25},{4,122},{5,31},{6,120},{7,29},{8,118... | collective-permute-start | bytes 2752520 | tf_op jit(solution)/shard_map/ppermute | solution.py:350
  99.3 1.3 collective-permute-start.8
  100.6 0.3 collective-permute-start.9
  101.0 23.2 %shard_map.131 = (bf16[128,3584]{1,0:T(8,128)(2,1)}, bf16[128,3584]{1,0:T(8,128)(2,1)}, bf16[128,3584]{1,0:T(8,128)(2,1)}, bf16[128,3584]{1,0:T(8,128)(2,1)}) custom-call(bf16[128,3584]{1,0:T(8,128)(2,1)} %copy-done.17, bf16[128,3584]{1,0:T(8,128)(2,1)} %copy-done.19, bf16[128,3584]{1,0:T(8,128)(2,1)} %collective-permute-done.18.refs_2_, ...), custom_call_target="tpu_custom_call" | custom-call | flops 11274289152 | bytes 31457280 | tf_op jit(solution)/shard_map/pallas_call | solution.py:279
  124.2 2.8 %collective-permute-start.20 = (bf16[128,3584]{1,0:T(8,128)(2,1)}, bf16[128,3584]{1,0:T(8,128)(2,1)S(1)}, u32[]{:S(2)}, u32[]{:S(2)}) collective-permute-start(bf16[128,3584]{1,0:T(8,128)(2,1)} %get-tuple-element.43), channel_id=1, source_target_pairs={{0,6},{1,3},{2,4},{3,1},{4,2},{5,7},{6,0},{7,5},{8,14},{9,11},{10,... | collective-permute-start | bytes 2752520 | tf_op jit(solution)/shard_map/ppermute | solution.py:350
  126.9 2.9 %collective-permute-start.21 = (bf16[128,3584]{1,0:T(8,128)(2,1)}, bf16[128,3584]{1,0:T(8,128)(2,1)S(1)}, u32[]{:S(2)}, u32[]{:S(2)}) collective-permute-start(bf16[128,3584]{1,0:T(8,128)(2,1)} %get-tuple-element.44), channel_id=1, source_target_pairs={{0,78},{1,11},{2,76},{3,9},{4,74},{5,15},{6,72},{7,13},{8,70},{9,3... | collective-permute-start | bytes 2752520 | tf_op jit(solution)/shard_map/ppermute | solution.py:350
  129.8 0.6 collective-permute-start.22
  130.4 1.3 collective-permute-start.23
  131.7 1.0 copy-done.18
  132.7 23.2 %shard_map.130 = (bf16[128,3584]{1,0:T(8,128)(2,1)}, bf16[128,3584]{1,0:T(8,128)(2,1)}, bf16[128,3584]{1,0:T(8,128)(2,1)}, bf16[128,3584]{1,0:T(8,128)(2,1)}) custom-call(bf16[128,3584]{1,0:T(8,128)(2,1)} %get-tuple-element.33.refs_0_, bf16[128,3584]{1,0:T(8,128)(2,1)} %copy-done.15, bf16[128,3584]{1,0:T(8,128)(2,1)} %copy-done.16, ...), custom_call_target="tpu_custom_call" | custom-call | flops 11274289152 | bytes 31457280 | tf_op jit(solution)/shard_map/pallas_call | solution.py:279
  155.9 2.9 %collective-permute-start.15 = (bf16[128,3584]{1,0:T(8,128)(2,1)}, bf16[128,3584]{1,0:T(8,128)(2,1)S(1)}, u32[]{:S(2)}, u32[]{:S(2)}) collective-permute-start(bf16[128,3584]{1,0:T(8,128)(2,1)} %get-tuple-element.38), channel_id=1, source_target_pairs={{0,72},{1,9},{2,74},{3,11},{4,76},{5,13},{6,78},{7,15},{8,64},{9,1... | collective-permute-start | bytes 2752520 | tf_op jit(solution)/shard_map/ppermute | solution.py:350
  158.8 2.8 %collective-permute-start.24 = (bf16[128,3584]{1,0:T(8,128)(2,1)}, bf16[128,3584]{1,0:T(8,128)(2,1)S(1)}, u32[]{:S(2)}, u32[]{:S(2)}) collective-permute-start(bf16[128,3584]{1,0:T(8,128)(2,1)} %get-tuple-element.47), channel_id=1, source_target_pairs={{0,54},{1,19},{2,52},{3,17},{4,50},{5,23},{6,48},{7,21},{8,62},{9,... | collective-permute-start | bytes 2752520 | tf_op jit(solution)/shard_map/ppermute | solution.py:350
  161.6 1.2 collective-permute-start.25
  162.8 7.2 %shard_map.128 = (bf16[8,128,128]{2,1,0:T(8,128)(2,1)}, bf16[8,128,128]{2,1,0:T(8,128)(2,1)}) custom-call(s32[8]{0:T(128)} %fusion.experts_ref, bf16[128,3712]{1,0:T(8,128)(2,1)} %shard_map.127.refs_0_.refs_8_, bf16[128,3712]{1,0:T(8,128)(2,1)} %collective-permute-done.refs_1_.refs_9_, bf16[128,3712]{1,0:T(8,128)(2,1)} %collective-permute-done.1.refs_2_.refs_10_, ...), custom_call_target="tpu_custom_call" | custom-call | bytes 4194304 | tf_op jit(solution)/shard_map/pallas_call | solution.py:205
  170.1 0.8 collective-permute-done.15.refs_1_
  170.9 3.6 %collective-permute-done.24.refs_6_ = bf16[128,3584]{1,0:T(8,128)(2,1)S(1)} collective-permute-done((bf16[128,3584]{1,0:T(8,128)(2,1)}, bf16[128,3584]{1,0:T(8,128)(2,1)S(1)}, u32[]{:S(2)}, u32[]{:S(2)}) %collective-permute-start.24) | collective-permute-done | bytes 917536 | tf_op jit(solution)/shard_map/ppermute | solution.py:350
  174.5 9.7 %collective-permute-done.25.refs_7_ = bf16[128,3584]{1,0:T(8,128)(2,1)S(1)} collective-permute-done((bf16[128,3584]{1,0:T(8,128)(2,1)}, bf16[128,3584]{1,0:T(8,128)(2,1)S(1)}, u32[]{:S(2)}, u32[]{:S(2)}) %collective-permute-start.25) | collective-permute-done | bytes 917536 | tf_op jit(solution)/shard_map/ppermute | solution.py:350
  184.2 0.9 copy-done.11
  185.2 10.3 %shard_map.132 = (f32[128,3584]{1,0:T(8,128)}, bf16[128,3584]{1,0:T(8,128)(2,1)}, bf16[128,3584]{1,0:T(8,128)(2,1)}, bf16[128,3584]{1,0:T(8,128)(2,1)}, bf16[128...) custom-call(bf16[8,128,128]{2,1,0:T(8,128)(2,1)} %get-tuple-element.31.hig, ...), custom_call_target="tpu_custom_call" | custom-call | flops 1879048192 | bytes 14680064 | tf_op jit(solution)/shard_map/pallas_call | solution.py:318
  195.4 0.1 collective-permute-start.26
  195.5 0.1 collective-permute-start.27
  195.6 3.4 %collective-permute-start.28 = (bf16[128,3584]{1,0:T(8,128)(2,1)}, bf16[128,3584]{1,0:T(8,128)(2,1)S(1)}, u32[]{:S(2)}, u32[]{:S(2)}) collective-permute-start(bf16[128,3584]{1,0:T(8,128)(2,1)} %get-tuple-element.52), channel_id=1, source_target_pairs={{0,10},{1,79},{2,8},{3,77},{4,14},{5,75},{6,12},{7,73},{8,2},{9,71... | collective-permute-start | bytes 2752520 | tf_op jit(solution)/shard_map/ppermute | solution.py:350
  199.0 6.9 %collective-permute-start.29 = (bf16[128,3584]{1,0:T(8,128)(2,1)}, bf16[128,3584]{1,0:T(8,128)(2,1)S(1)}, u32[]{:S(2)}, u32[]{:S(2)}) collective-permute-start(bf16[128,3584]{1,0:T(8,128)(2,1)} %get-tuple-element.53), channel_id=1, source_target_pairs={{0,16},{1,49},{2,18},{3,51},{4,20},{5,53},{6,22},{7,55},{8,24},{9,... | collective-permute-start | bytes 2752520 | tf_op jit(solution)/shard_map/ppermute | solution.py:350
  205.9 3.3 %collective-permute-done.26 = bf16[128,3584]{1,0:T(8,128)(2,1)S(1)} collective-permute-done((bf16[128,3584]{1,0:T(8,128)(2,1)}, bf16[128,3584]{1,0:T(8,128)(2,1)S(1)}, u32[]{:S(2)}, u32[]{:S(2)}) %collective-permute-start.26) | collective-permute-done | bytes 917536 | tf_op jit(solution)/shard_map/ppermute | solution.py:350
  209.1 1.9 collective-permute-start.31
  211.0 5.9 %collective-permute-start.32 = (bf16[128,3584]{1,0:T(8,128)(2,1)}, bf16[128,3584]{1,0:T(8,128)(2,1)S(1)}, u32[]{:S(2)}, u32[]{:S(2)}) collective-permute-start(bf16[128,3584]{1,0:T(8,128)(2,1)} %get-tuple-element.56), channel_id=1, source_target_pairs={{0,26},{1,127},{2,24},{3,125},{4,30},{5,123},{6,28},{7,121},{8,18}... | collective-permute-start | bytes 2752520 | tf_op jit(solution)/shard_map/ppermute | solution.py:350
  216.9 7.0 %collective-permute-done.28 = bf16[128,3584]{1,0:T(8,128)(2,1)S(1)} collective-permute-done((bf16[128,3584]{1,0:T(8,128)(2,1)}, bf16[128,3584]{1,0:T(8,128)(2,1)S(1)}, u32[]{:S(2)}, u32[]{:S(2)}) %collective-permute-start.28) | collective-permute-done | bytes 917536 | tf_op jit(solution)/shard_map/ppermute | solution.py:350
  223.9 9.4 %collective-permute-done.30 = bf16[128,3584]{1,0:T(8,128)(2,1)S(1)} collective-permute-done((bf16[128,3584]{1,0:T(8,128)(2,1)}, bf16[128,3584]{1,0:T(8,128)(2,1)S(1)}, u32[]{:S(2)}, u32[]{:S(2)}) %collective-permute-start.30) | collective-permute-done | bytes 917536 | tf_op jit(solution)/shard_map/ppermute | solution.py:350
  233.3 9.8 %collective-permute-done.31 = bf16[128,3584]{1,0:T(8,128)(2,1)S(1)} collective-permute-done((bf16[128,3584]{1,0:T(8,128)(2,1)}, bf16[128,3584]{1,0:T(8,128)(2,1)S(1)}, u32[]{:S(2)}, u32[]{:S(2)}) %collective-permute-start.31) | collective-permute-done | bytes 917536 | tf_op jit(solution)/shard_map/ppermute | solution.py:350
  243.1 9.8 %collective-permute-done.32 = bf16[128,3584]{1,0:T(8,128)(2,1)S(1)} collective-permute-done((bf16[128,3584]{1,0:T(8,128)(2,1)}, bf16[128,3584]{1,0:T(8,128)(2,1)S(1)}, u32[]{:S(2)}, u32[]{:S(2)}) %collective-permute-start.32) | collective-permute-done | bytes 917536 | tf_op jit(solution)/shard_map/ppermute | solution.py:350
  253.0 3.6 %add_convert_fusion = bf16[128,3584]{1,0:T(8,128)(2,1)} fusion(bf16[128,3584]{1,0:T(8,128)(2,1)S(1)} %collective-permute-done.32, bf16[128,3584]{1,0:T(8,128)(2,1)S(1)} %collective-permute-done.31, bf16[128,3584]{1,0:T(8,128)(2,1)S(1)} %collective-permute-done.30, bf16[128,3584]{1,0:T(8,128)(2,1)S(1)} %collective-permute-done.29, ...), kind=kLoop, calls=%fused_computation.4 | loop fusion | flops 6881280 | bytes 9175040 | tf_op jit(solution)/shard_map/convert_element_type | solution.py:392
  (57 shorter events, 0.1 us)
Async XLA Ops:
  0.0 40.0 %copy-start = (bf16[1,2048,512]{2,1,0:T(8,128)(2,1)S(1)}, bf16[1,2048,512]{2,1,0:T(8,128)(2,1)}, u32[]{:S(2)}) copy-start(bf16[1,2048,512]{2,1,0:T(8,128)(2,1)} %param.19) | copy-start | bytes 6291460
  2.8 14.0 %collective-permute-start.3 = (bf16[128,3712]{1,0:T(8,128)(2,1)}, bf16[128,3712]{1,0:T(8,128)(2,1)S(1)}, u32[]{:S(2)}, u32[]{:S(2)}) collective-permute-start(bf16[128,3712]{1,0:T(8,128)(2,1)} %shard_map.127.refs_0_.refs_8_), channel_id=1, source_target_pairs={{0,16},{1,49},{2,18},{3,51},{4,20},{5,53},{6,22},{7,55},{8,24},{9,... | collective-permute-start | bytes 2850824 | tf_op jit(solution)/shard_map/ppermute | solution.py:350
  4.0 24.2 %collective-permute-start.1 = (bf16[128,3712]{1,0:T(8,128)(2,1)}, bf16[128,3712]{1,0:T(8,128)(2,1)}, u32[]{:S(2)}, u32[]{:S(2)}) collective-permute-start(bf16[128,3712]{1,0:T(8,128)(2,1)} %shard_map.127.refs_0_.refs_8_), channel_id=1, source_target_pairs={{0,2},{1,7},{2,0},{3,5},{4,6},{5,3},{6,4},{7,1},{8,10},{9,15},{10,... | collective-permute-start | bytes 2850824 | tf_op jit(solution)/shard_map/ppermute | solution.py:350
  5.5 24.6 %collective-permute-start = (bf16[128,3712]{1,0:T(8,128)(2,1)}, bf16[128,3712]{1,0:T(8,128)(2,1)}, u32[]{:S(2)}, u32[]{:S(2)}) collective-permute-start(bf16[128,3712]{1,0:T(8,128)(2,1)} %shard_map.127.refs_0_.refs_8_), channel_id=1, source_target_pairs={{0,8},{1,73},{2,10},{3,75},{4,12},{5,77},{6,14},{7,79},{8,0},{9,65... | collective-permute-start | bytes 2850824 | tf_op jit(solution)/shard_map/ppermute | solution.py:350
  7.4 24.8 %collective-permute-start.6 = (bf16[128,3712]{1,0:T(8,128)(2,1)}, bf16[128,3712]{1,0:T(8,128)(2,1)S(1)}, u32[]{:S(2)}, u32[]{:S(2)}) collective-permute-start(bf16[128,3712]{1,0:T(8,128)(2,1)} %shard_map.127.refs_0_.refs_8_), channel_id=1, source_target_pairs={{0,26},{1,127},{2,24},{3,125},{4,30},{5,123},{6,28},{7,121},{8,18}... | collective-permute-start | bytes 2850824 | tf_op jit(solution)/shard_map/ppermute | solution.py:350
  16.7 28.1 %copy-start.2 = (bf16[128,3712]{1,0:T(8,128)(2,1)}, bf16[128,3712]{1,0:T(8,128)(2,1)S(1)}, u32[]{:S(2)}) copy-start(bf16[128,3712]{1,0:T(8,128)(2,1)S(1)} %collective-permute-done.3.refs_4_.refs_12_) | copy-start | bytes 2850820
  16.7 21.6 %collective-permute-start.5 = (bf16[128,3712]{1,0:T(8,128)(2,1)S(1)}, bf16[128,3712]{1,0:T(8,128)(2,1)S(1)}, u32[]{:S(2)}, u32[]{:S(2)}) collective-permute-start(bf16[128,3712]{1,0:T(8,128)(2,1)S(1)} %collective-permute-done.3.refs_4_.refs_12_), channel_id=1, source_target_pairs={{0,2},{1,7},{2,0},{3,5},{4,6},{5,3},{6,4},{7,1},{8,10},{9,15},{10,... | collective-permute-start | bytes 2850824 | tf_op jit(solution)/shard_map/ppermute | solution.py:350
  28.2 16.6 %collective-permute-start.2 = (bf16[128,3712]{1,0:T(8,128)(2,1)}, bf16[128,3712]{1,0:T(8,128)(2,1)}, u32[]{:S(2)}, u32[]{:S(2)}) collective-permute-start(bf16[128,3712]{1,0:T(8,128)(2,1)} %collective-permute-done.1.refs_2_.refs_10_), channel_id=1, source_target_pairs={{0,8},{1,73},{2,10},{3,75},{4,12},{5,77},{6,14},{7,79},{8,0},{9,65... | collective-permute-start | bytes 2850824 | tf_op jit(solution)/shard_map/ppermute | solution.py:350
  30.1 15.2 %collective-permute-start.4 = (bf16[128,3712]{1,0:T(8,128)(2,1)}, bf16[128,3712]{1,0:T(8,128)(2,1)}, u32[]{:S(2)}, u32[]{:S(2)}) collective-permute-start(bf16[128,3712]{1,0:T(8,128)(2,1)} %collective-permute-done.refs_1_.refs_9_), channel_id=1, source_target_pairs={{0,16},{1,49},{2,18},{3,51},{4,20},{5,53},{6,22},{7,55},{8,24},{9,... | collective-permute-start | bytes 2850824 | tf_op jit(solution)/shard_map/ppermute | solution.py:350
  30.1 70.5 %collective-permute-start.13 = (bf16[3584,512]{1,0:T(8,128)(2,1)}, bf16[3584,512]{1,0:T(8,128)(2,1)}, u32[]{:S(2)}, u32[]{:S(2)}) collective-permute-start(bf16[3584,512]{1,0:T(8,128)(2,1)} %bitcast.48), channel_id=1, source_target_pairs={{0,1},{1,0},{2,3},{3,2},{4,5},{5,4},{6,7},{7,6},{8,9},{9,8},{10,11... | collective-permute-start | bytes 11010056 | tf_op jit(solution)/shard_map/ppermute | solution.py:356
  32.2 6.1 %copy-start.3 = (bf16[128,3712]{1,0:T(8,128)(2,1)}, bf16[128,3712]{1,0:T(8,128)(2,1)S(1)}, u32[]{:S(2)}) copy-start(bf16[128,3712]{1,0:T(8,128)(2,1)S(1)} %collective-permute-done.6.refs_7_.refs_15_) | copy-start | bytes 2850820
  32.2 68.7 %collective-permute-start.14 = (bf16[3584,512]{1,0:T(8,128)(2,1)}, bf16[3584,512]{1,0:T(8,128)(2,1)}, u32[]{:S(2)}, u32[]{:S(2)}) collective-permute-start(bf16[3584,512]{1,0:T(8,128)(2,1)} %bitcast.51), channel_id=1, source_target_pairs={{0,1},{1,0},{2,3},{3,2},{4,5},{5,4},{6,7},{7,6},{8,9},{9,8},{10,11... | collective-permute-start | bytes 11010056 | tf_op jit(solution)/shard_map/ppermute | solution.py:356
  38.3 1.0 copy-start.4
  39.2 61.7 %collective-permute-start.12 = (bf16[512,3584]{1,0:T(8,128)(2,1)}, bf16[512,3584]{1,0:T(8,128)(2,1)}, u32[]{:S(2)}, u32[]{:S(2)}) collective-permute-start(bf16[512,3584]{1,0:T(8,128)(2,1)} %bitcast.45), channel_id=1, source_target_pairs={{0,1},{1,0},{2,3},{3,2},{4,5},{5,4},{6,7},{7,6},{8,9},{9,8},{10,11... | collective-permute-start | bytes 11010056 | tf_op jit(solution)/shard_map/ppermute | solution.py:356
  44.8 15.3 %collective-permute-start.10 = (bf16[1024,512]{1,0:T(8,128)(2,1)}, bf16[1024,512]{1,0:T(8,128)(2,1)S(1)}, u32[]{:S(2)}, u32[]{:S(2)}) collective-permute-start(bf16[1024,512]{1,0:T(8,128)(2,1)} %bitcast.40), channel_id=1, source_target_pairs={{0,1},{1,0},{2,3},{3,2},{4,5},{5,4},{6,7},{7,6},{8,9},{9,8},{10,11... | collective-permute-start | bytes 3145736 | tf_op jit(solution)/shard_map/ppermute | solution.py:356
  45.3 21.4 %collective-permute-start.11 = (bf16[1024,512]{1,0:T(8,128)(2,1)}, bf16[1024,512]{1,0:T(8,128)(2,1)S(1)}, u32[]{:S(2)}, u32[]{:S(2)}) collective-permute-start(bf16[1024,512]{1,0:T(8,128)(2,1)} %bitcast.39), channel_id=1, source_target_pairs={{0,1},{1,0},{2,3},{3,2},{4,5},{5,4},{6,7},{7,6},{8,9},{9,8},{10,11... | collective-permute-start | bytes 3145736 | tf_op jit(solution)/shard_map/ppermute | solution.py:356
  60.2 23.9 %copy-start.12 = (bf16[1024,512]{1,0:T(8,128)(2,1)}, bf16[1024,512]{1,0:T(8,128)(2,1)S(1)}, u32[]{:S(2)}) copy-start(bf16[1024,512]{1,0:T(8,128)(2,1)S(1)} %collective-permute-done.10.refs_6_) | copy-start | bytes 3145732
  60.2 18.2 %collective-permute-start.16 = (bf16[128,3584]{1,0:T(8,128)(2,1)}, bf16[128,3584]{1,0:T(8,128)(2,1)S(1)}, u32[]{:S(2)}, u32[]{:S(2)}) collective-permute-start(bf16[128,3584]{1,0:T(8,128)(2,1)} %get-tuple-element.39), channel_id=1, source_target_pairs={{0,78},{1,11},{2,76},{3,9},{4,74},{5,15},{6,72},{7,13},{8,70},{9,3... | collective-permute-start | bytes 2752520 | tf_op jit(solution)/shard_map/ppermute | solution.py:350
  66.7 17.3 %copy-start.13 = (bf16[1024,512]{1,0:T(8,128)(2,1)}, bf16[1024,512]{1,0:T(8,128)(2,1)S(1)}, u32[]{:S(2)}) copy-start(bf16[1024,512]{1,0:T(8,128)(2,1)S(1)} %collective-permute-done.11.refs_7_) | copy-start | bytes 3145732
  66.7 14.4 %collective-permute-start.17 = (bf16[128,3584]{1,0:T(8,128)(2,1)}, bf16[128,3584]{1,0:T(8,128)(2,1)S(1)}, u32[]{:S(2)}, u32[]{:S(2)}) collective-permute-start(bf16[128,3584]{1,0:T(8,128)(2,1)} %get-tuple-element.40), channel_id=1, source_target_pairs={{0,48},{1,17},{2,50},{3,19},{4,52},{5,21},{6,54},{7,23},{8,56},{9,... | collective-permute-start | bytes 2752520 | tf_op jit(solution)/shard_map/ppermute | solution.py:350
  78.3 5.7 %copy-start.17 = (bf16[128,3584]{1,0:T(8,128)(2,1)}, bf16[128,3584]{1,0:T(8,128)(2,1)S(1)}, u32[]{:S(2)}) copy-start(bf16[128,3584]{1,0:T(8,128)(2,1)S(1)} %collective-permute-done.16.refs_0_) | copy-start | bytes 2752516
  78.3 15.8 %collective-permute-start.18 = (bf16[128,3584]{1,0:T(8,128)(2,1)}, bf16[128,3584]{1,0:T(8,128)(2,1)}, u32[]{:S(2)}, u32[]{:S(2)}) collective-permute-start(bf16[128,3584]{1,0:T(8,128)(2,1)} %get-tuple-element.41), channel_id=1, source_target_pairs={{0,120},{1,25},{2,122},{3,27},{4,124},{5,29},{6,126},{7,31},{8,112... | collective-permute-start | bytes 2752520 | tf_op jit(solution)/shard_map/ppermute | solution.py:350
  81.1 2.9 %copy-start.19 = (bf16[128,3584]{1,0:T(8,128)(2,1)}, bf16[128,3584]{1,0:T(8,128)(2,1)S(1)}, u32[]{:S(2)}) copy-start(bf16[128,3584]{1,0:T(8,128)(2,1)S(1)} %collective-permute-done.17.refs_1_) | copy-start | bytes 2752516
  81.1 18.2 %collective-permute-start.19 = (bf16[128,3584]{1,0:T(8,128)(2,1)}, bf16[128,3584]{1,0:T(8,128)(2,1)}, u32[]{:S(2)}, u32[]{:S(2)}) collective-permute-start(bf16[128,3584]{1,0:T(8,128)(2,1)} %get-tuple-element.42), channel_id=1, source_target_pairs={{0,6},{1,3},{2,4},{3,1},{4,2},{5,7},{6,0},{7,5},{8,14},{9,11},{10,... | collective-permute-start | bytes 2752520 | tf_op jit(solution)/shard_map/ppermute | solution.py:350
  84.0 16.6 %copy-start.14 = (bf16[128,3584]{1,0:T(8,128)(2,1)S(1)}, bf16[128,3584]{1,0:T(8,128)(2,1)}, u32[]{:S(2)}) copy-start(bf16[128,3584]{1,0:T(8,128)(2,1)} %get-tuple-element.36) | copy-start | bytes 2752516
  94.1 35.7 %collective-permute-start.7 = (bf16[128,3584]{1,0:T(8,128)(2,1)}, bf16[128,3584]{1,0:T(8,128)(2,1)S(1)}, u32[]{:S(2)}, u32[]{:S(2)}) collective-permute-start(bf16[128,3584]{1,0:T(8,128)(2,1)} %get-tuple-element.34), channel_id=1, source_target_pairs={{0,126},{1,27},{2,124},{3,25},{4,122},{5,31},{6,120},{7,29},{8,118... | collective-permute-start | bytes 2752520 | tf_op jit(solution)/shard_map/ppermute | solution.py:350
  99.3 31.2 %collective-permute-start.8 = (bf16[128,3584]{1,0:T(8,128)(2,1)}, bf16[128,3584]{1,0:T(8,128)(2,1)S(1)}, u32[]{:S(2)}, u32[]{:S(2)}) collective-permute-start(bf16[128,3584]{1,0:T(8,128)(2,1)} %get-tuple-element.35), channel_id=1, source_target_pairs={{0,54},{1,19},{2,52},{3,17},{4,50},{5,23},{6,48},{7,21},{8,62},{9,... | collective-permute-start | bytes 2752520 | tf_op jit(solution)/shard_map/ppermute | solution.py:350
  100.6 31.1 %collective-permute-start.9 = (bf16[128,3584]{1,0:T(8,128)(2,1)S(1)}, bf16[128,3584]{1,0:T(8,128)(2,1)S(1)}, u32[]{:S(2)}, u32[]{:S(2)}) collective-permute-start(bf16[128,3584]{1,0:T(8,128)(2,1)S(1)} %copy-done.14), channel_id=1, source_target_pairs={{0,72},{1,9},{2,74},{3,11},{4,76},{5,13},{6,78},{7,15},{8,64},{9,1... | collective-permute-start | bytes 2752520 | tf_op jit(solution)/shard_map/ppermute | solution.py:350
  124.2 34.6 %collective-permute-start.20 = (bf16[128,3584]{1,0:T(8,128)(2,1)}, bf16[128,3584]{1,0:T(8,128)(2,1)S(1)}, u32[]{:S(2)}, u32[]{:S(2)}) collective-permute-start(bf16[128,3584]{1,0:T(8,128)(2,1)} %get-tuple-element.43), channel_id=1, source_target_pairs={{0,6},{1,3},{2,4},{3,1},{4,2},{5,7},{6,0},{7,5},{8,14},{9,11},{10,... | collective-permute-start | bytes 2752520 | tf_op jit(solution)/shard_map/ppermute | solution.py:350
  126.9 34.7 %collective-permute-start.21 = (bf16[128,3584]{1,0:T(8,128)(2,1)}, bf16[128,3584]{1,0:T(8,128)(2,1)S(1)}, u32[]{:S(2)}, u32[]{:S(2)}) collective-permute-start(bf16[128,3584]{1,0:T(8,128)(2,1)} %get-tuple-element.44), channel_id=1, source_target_pairs={{0,78},{1,11},{2,76},{3,9},{4,74},{5,15},{6,72},{7,13},{8,70},{9,3... | collective-permute-start | bytes 2752520 | tf_op jit(solution)/shard_map/ppermute | solution.py:350
  129.8 1.9 copy-start.15
  129.8 40.2 %collective-permute-start.22 = (bf16[128,3584]{1,0:T(8,128)(2,1)}, bf16[128,3584]{1,0:T(8,128)(2,1)S(1)}, u32[]{:S(2)}, u32[]{:S(2)}) collective-permute-start(bf16[128,3584]{1,0:T(8,128)(2,1)} %get-tuple-element.45), channel_id=1, source_target_pairs={{0,48},{1,17},{2,50},{3,19},{4,52},{5,21},{6,54},{7,23},{8,56},{9,... | collective-permute-start | bytes 2752520 | tf_op jit(solution)/shard_map/ppermute | solution.py:350
  130.4 1.3 copy-start.16
  130.4 39.6 %collective-permute-start.23 = (bf16[128,3584]{1,0:T(8,128)(2,1)}, bf16[128,3584]{1,0:T(8,128)(2,1)S(1)}, u32[]{:S(2)}, u32[]{:S(2)}) collective-permute-start(bf16[128,3584]{1,0:T(8,128)(2,1)} %get-tuple-element.46), channel_id=1, source_target_pairs={{0,120},{1,25},{2,122},{3,27},{4,124},{5,29},{6,126},{7,31},{8,112... | collective-permute-start | bytes 2752520 | tf_op jit(solution)/shard_map/ppermute | solution.py:350
  131.7 1.0 copy-start.18
  155.9 15.0 %collective-permute-start.15 = (bf16[128,3584]{1,0:T(8,128)(2,1)}, bf16[128,3584]{1,0:T(8,128)(2,1)S(1)}, u32[]{:S(2)}, u32[]{:S(2)}) collective-permute-start(bf16[128,3584]{1,0:T(8,128)(2,1)} %get-tuple-element.38), channel_id=1, source_target_pairs={{0,72},{1,9},{2,74},{3,11},{4,76},{5,13},{6,78},{7,15},{8,64},{9,1... | collective-permute-start | bytes 2752520 | tf_op jit(solution)/shard_map/ppermute | solution.py:350
  158.8 11.2 %copy-start.5 = (bf16[128,3584]{1,0:T(8,128)(2,1)}, bf16[128,3584]{1,0:T(8,128)(2,1)S(1)}, u32[]{:S(2)}) copy-start(bf16[128,3584]{1,0:T(8,128)(2,1)S(1)} %collective-permute-done.20.refs_2_) | copy-start | bytes 2752516
  158.8 15.7 %collective-permute-start.24 = (bf16[128,3584]{1,0:T(8,128)(2,1)}, bf16[128,3584]{1,0:T(8,128)(2,1)S(1)}, u32[]{:S(2)}, u32[]{:S(2)}) collective-permute-start(bf16[128,3584]{1,0:T(8,128)(2,1)} %get-tuple-element.47), channel_id=1, source_target_pairs={{0,54},{1,19},{2,52},{3,17},{4,50},{5,23},{6,48},{7,21},{8,62},{9,... | collective-permute-start | bytes 2752520 | tf_op jit(solution)/shard_map/ppermute | solution.py:350
  161.6 8.4 %copy-start.6 = (bf16[128,3584]{1,0:T(8,128)(2,1)}, bf16[128,3584]{1,0:T(8,128)(2,1)S(1)}, u32[]{:S(2)}) copy-start(bf16[128,3584]{1,0:T(8,128)(2,1)S(1)} %collective-permute-done.21.refs_3_) | copy-start | bytes 2752516
  161.6 22.6 %collective-permute-start.25 = (bf16[128,3584]{1,0:T(8,128)(2,1)}, bf16[128,3584]{1,0:T(8,128)(2,1)S(1)}, u32[]{:S(2)}, u32[]{:S(2)}) collective-permute-start(bf16[128,3584]{1,0:T(8,128)(2,1)} %get-tuple-element.48), channel_id=1, source_target_pairs={{0,126},{1,27},{2,124},{3,25},{4,122},{5,31},{6,120},{7,29},{8,118... | collective-permute-start | bytes 2752520 | tf_op jit(solution)/shard_map/ppermute | solution.py:350
  170.0 14.2 %copy-start.7 = (bf16[128,3584]{1,0:T(8,128)(2,1)}, bf16[128,3584]{1,0:T(8,128)(2,1)S(1)}, u32[]{:S(2)}) copy-start(bf16[128,3584]{1,0:T(8,128)(2,1)S(1)} %collective-permute-done.22.refs_4_) | copy-start | bytes 2752516
  170.0 14.2 %copy-start.8 = (bf16[128,3584]{1,0:T(8,128)(2,1)}, bf16[128,3584]{1,0:T(8,128)(2,1)S(1)}, u32[]{:S(2)}) copy-start(bf16[128,3584]{1,0:T(8,128)(2,1)S(1)} %collective-permute-done.23.refs_5_) | copy-start | bytes 2752516
  170.9 13.3 %copy-start.9 = (bf16[128,3584]{1,0:T(8,128)(2,1)}, bf16[128,3584]{1,0:T(8,128)(2,1)S(1)}, u32[]{:S(2)}) copy-start(bf16[128,3584]{1,0:T(8,128)(2,1)S(1)} %collective-permute-done.15.refs_1_) | copy-start | bytes 2752516
  174.5 9.7 %copy-start.10 = (bf16[128,3584]{1,0:T(8,128)(2,1)}, bf16[128,3584]{1,0:T(8,128)(2,1)S(1)}, u32[]{:S(2)}) copy-start(bf16[128,3584]{1,0:T(8,128)(2,1)S(1)} %collective-permute-done.24.refs_6_) | copy-start | bytes 2752516
  184.2 1.0 copy-start.11
  195.4 13.7 %collective-permute-start.26 = (bf16[128,3584]{1,0:T(8,128)(2,1)}, bf16[128,3584]{1,0:T(8,128)(2,1)S(1)}, u32[]{:S(2)}, u32[]{:S(2)}) collective-permute-start(bf16[128,3584]{1,0:T(8,128)(2,1)} %get-tuple-element.50), channel_id=1, source_target_pairs={{0,8},{1,73},{2,10},{3,75},{4,12},{5,77},{6,14},{7,79},{8,0},{9,65... | collective-permute-start | bytes 2752520 | tf_op jit(solution)/shard_map/ppermute | solution.py:350
  195.5 15.4 %collective-permute-start.27 = (bf16[128,3584]{1,0:T(8,128)(2,1)}, bf16[128,3584]{1,0:T(8,128)(2,1)S(1)}, u32[]{:S(2)}, u32[]{:S(2)}) collective-permute-start(bf16[128,3584]{1,0:T(8,128)(2,1)} %get-tuple-element.51), channel_id=1, source_target_pairs={{0,2},{1,7},{2,0},{3,5},{4,6},{5,3},{6,4},{7,1},{8,10},{9,15},{10,... | collective-permute-start | bytes 2752520 | tf_op jit(solution)/shard_map/ppermute | solution.py:350
  195.6 28.2 %collective-permute-start.28 = (bf16[128,3584]{1,0:T(8,128)(2,1)}, bf16[128,3584]{1,0:T(8,128)(2,1)S(1)}, u32[]{:S(2)}, u32[]{:S(2)}) collective-permute-start(bf16[128,3584]{1,0:T(8,128)(2,1)} %get-tuple-element.52), channel_id=1, source_target_pairs={{0,10},{1,79},{2,8},{3,77},{4,14},{5,75},{6,12},{7,73},{8,2},{9,71... | collective-permute-start | bytes 2752520 | tf_op jit(solution)/shard_map/ppermute | solution.py:350
  199.0 24.9 %collective-permute-start.29 = (bf16[128,3584]{1,0:T(8,128)(2,1)}, bf16[128,3584]{1,0:T(8,128)(2,1)S(1)}, u32[]{:S(2)}, u32[]{:S(2)}) collective-permute-start(bf16[128,3584]{1,0:T(8,128)(2,1)} %get-tuple-element.53), channel_id=1, source_target_pairs={{0,16},{1,49},{2,18},{3,51},{4,20},{5,53},{6,22},{7,55},{8,24},{9,... | collective-permute-start | bytes 2752520 | tf_op jit(solution)/shard_map/ppermute | solution.py:350
  205.9 27.4 %collective-permute-start.30 = (bf16[128,3584]{1,0:T(8,128)(2,1)}, bf16[128,3584]{1,0:T(8,128)(2,1)S(1)}, u32[]{:S(2)}, u32[]{:S(2)}) collective-permute-start(bf16[128,3584]{1,0:T(8,128)(2,1)} %get-tuple-element.54), channel_id=1, source_target_pairs={{0,24},{1,121},{2,26},{3,123},{4,28},{5,125},{6,30},{7,127},{8,16}... | collective-permute-start | bytes 2752520 | tf_op jit(solution)/shard_map/ppermute | solution.py:350
  209.1 34.0 %collective-permute-start.31 = (bf16[128,3584]{1,0:T(8,128)(2,1)}, bf16[128,3584]{1,0:T(8,128)(2,1)S(1)}, u32[]{:S(2)}, u32[]{:S(2)}) collective-permute-start(bf16[128,3584]{1,0:T(8,128)(2,1)} %get-tuple-element.55), channel_id=1, source_target_pairs={{0,18},{1,55},{2,16},{3,53},{4,22},{5,51},{6,20},{7,49},{8,26},{9,... | collective-permute-start | bytes 2752520 | tf_op jit(solution)/shard_map/ppermute | solution.py:350
  211.0 42.0 %collective-permute-start.32 = (bf16[128,3584]{1,0:T(8,128)(2,1)}, bf16[128,3584]{1,0:T(8,128)(2,1)S(1)}, u32[]{:S(2)}, u32[]{:S(2)}) collective-permute-start(bf16[128,3584]{1,0:T(8,128)(2,1)} %get-tuple-element.56), channel_id=1, source_target_pairs={{0,26},{1,127},{2,24},{3,125},{4,30},{5,123},{6,28},{7,121},{8,18}... | collective-permute-start | bytes 2752520 | tf_op jit(solution)/shard_map/ppermute | solution.py:350
  253.0 3.6 %copy-start.1 = (bf16[1,2048,512]{2,1,0:T(8,128)(2,1)S(1)}, bf16[1,2048,512]{2,1,0:T(8,128)(2,1)}, u32[]{:S(2)}) copy-start(bf16[1,2048,512]{2,1,0:T(8,128)(2,1)} %param.19) | copy-start | bytes 6291460
